TPU v7x, 32 devices: a whole 2x2x4 slice. The times are simulated.
32 devices in a mesh: batch: 4 (over x, core), head: 8 (over z, y).
Axes of the slice: x: 2, y: 2, z: 4, core: 2. Of those that a mesh axis runs over, the one named last changes fastest.
Arguments:
- token_ids: int32 [4, 2048], P('batch'), may hold values from 0 to 50303
- next_target: int32 [4, 2048], P('batch'), may hold values from 0 to 50303
- second_target: int32 [4, 2048], P('batch'), may hold values from 0 to 50303
- live_mask: int32 [4, 2048], P('batch'), may hold values 0 or 1
- row_lengths: int32 [4], P('batch'), may hold values from 1024 to 2048, as said below
- tables: float32 [3, 50304, 1024], P(None, 'head', 'batch'), may hold values from -0.65625 to 0.65625
- factor_head: float32 [1024, 160], P('batch', 'head'), may hold values from -0.375 to 0.375
- factor_shared: float32 [1024, 640], P('batch'), may hold values from -0.1875 to 0.1875
- project_out: float32 [1024, 1024], P('head', 'batch'), may hold values from -0.75 to 0.75
- feed_in: float32 [2, 1024, 2816], P(None, 'batch', 'head'), may hold values from -0.1875 to 0.1875
- feed_out: float32 [2816, 1024], P('head', 'batch'), may hold values from -0.109375 to 0.109375
- norm_gains: float32 [3, 1024], P(None, 'batch'), may hold values from 0.5 to 1.5
- tables_first: float32 [3, 50304, 1024], P(None, 'head', 'batch'), may hold values from -9.536743e-07 to 9.536743e-07
- factor_head_first: float32 [1024, 160], P('batch', 'head'), may hold values from -9.536743e-07 to 9.536743e-07
- factor_shared_first: float32 [1024, 640], P('batch'), may hold values from -9.536743e-07 to 9.536743e-07
- project_out_first: float32 [1024, 1024], P('head', 'batch'), may hold values from -9.536743e-07 to 9.536743e-07
- feed_in_first: float32 [2, 1024, 2816], P(None, 'batch', 'head'), may hold values from -9.536743e-07 to 9.536743e-07
- feed_out_first: float32 [2816, 1024], P('head', 'batch'), may hold values from -9.536743e-07 to 9.536743e-07
- norm_gains_first: float32 [3, 1024], P(None, 'batch'), may hold values from -3.8146973e-06 to 3.8146973e-06
- tables_second: float32 [3, 50304, 1024], P(None, 'head', 'batch'), may hold values from 7.270282e-14 to 9.69371e-13
- factor_head_second: float32 [1024, 160], P('batch', 'head'), may hold values from 7.270282e-14 to 9.69371e-13
- factor_shared_second: float32 [1024, 640], P('batch'), may hold values from 7.270282e-14 to 9.69371e-13
- project_out_second: float32 [1024, 1024], P('head', 'batch'), may hold values from 7.270282e-14 to 9.69371e-13
- feed_in_second: float32 [2, 1024, 2816], P(None, 'batch', 'head'), may hold values from 7.270282e-14 to 9.69371e-13
- feed_out_second: float32 [2816, 1024], P('head', 'batch'), may hold values from 7.270282e-14 to 9.69371e-13
- norm_gains_second: float32 [3, 1024], P(None, 'batch'), may hold values from 1.1632452e-12 to 1.5509935e-11
Outputs:
- loss: float32 [], replicated
- grad_norm: float32 [], replicated
- new_tables: float32 [3, 50304, 1024], P(None, 'head', 'batch')
- new_tables_first: float32 [3, 50304, 1024], P(None, 'head', 'batch')
- new_tables_second: float32 [3, 50304, 1024], P(None, 'head', 'batch')
- new_factor_head: float32 [1024, 160], P('batch', 'head')
- new_factor_head_first: float32 [1024, 160], P('batch', 'head')
- new_factor_head_second: float32 [1024, 160], P('batch', 'head')
- new_factor_shared: float32 [1024, 640], P('batch')
- new_factor_shared_first: float32 [1024, 640], P('batch')
- new_factor_shared_second: float32 [1024, 640], P('batch')
- new_project_out: float32 [1024, 1024], P('head', 'batch')
- new_project_out_first: float32 [1024, 1024], P('head', 'batch')
- new_project_out_second: float32 [1024, 1024], P('head', 'batch')
- new_feed_in: float32 [2, 1024, 2816], P(None, 'batch', 'head')
- new_feed_in_first: float32 [2, 1024, 2816], P(None, 'batch', 'head')
- new_feed_in_second: float32 [2, 1024, 2816], P(None, 'batch', 'head')
- new_feed_out: float32 [2816, 1024], P('head', 'batch')
- new_feed_out_first: float32 [2816, 1024], P('head', 'batch')
- new_feed_out_second: float32 [2816, 1024], P('head', 'batch')
- new_norm_gains: float32 [3, 1024], P(None, 'batch')
- new_norm_gains_first: float32 [3, 1024], P(None, 'batch')
- new_norm_gains_second: float32 [3, 1024], P(None, 'batch')
Inputs may be any that keep to these rules, and one draw needn't show every extreme that they name: `row_lengths`: each row's length is 2048 or 1024, and each of the two occurs in every draw.
All inputs are finite; a program needn't handle non-finite values. No bound on the sum of `live_mask` on one device may be relied on, other than what follows from the above.
Results may differ from a plain program's by a relative error of at most 0.02.
The roundings to bfloat16 on the way count: a program that leaves them out, or rounds other values in their place, can miss the bound.
Values may be sent and summed in bfloat16 or wider, within the bound.
No kernel may reach another device: no remote copies, remote signals or barrier semaphores. Data moves between devices by JAX's collectives and lax.ppermute only.
A program may use at most 512 MiB of HBM per device.

v0:
```python
import math

import jax
import jax.numpy as jnp
from jax import lax
from jax.sharding import PartitionSpec as P

DH = 64
RQ = 6
RK = 2
STEP = 10


HIGH = lax.Precision.HIGHEST
EPS = 1e-05
NEG = -1e30
CLIP = 0.02
BETA_ONE = 0.9
BETA_TWO = 0.95
ADAM_EPS = 1e-08
RATES = (0.1, 0.1, 0.05, 0.2, 0.05, 0.03, 0.3)
DECAYS = (0.1, 0.1, 0.1, 0.1, 0.1, 0.1, 0.0)
OWNED = (True, True, False, True, True, True, False)


def joined(value, axis, join):
    pieces = jax.tree.map(lambda part: lax.all_gather(part, axis), value)
    head = jax.tree.map(lambda part: part[0], pieces)
    tail = jax.tree.map(lambda part: part[1:], pieces)
    total, _ = lax.scan(lambda total, slab: (join(total, slab), None), head, tail)
    return total


def rms_norm(values, gain_row):
    return values * lax.rsqrt(jnp.mean(values * values, axis=-1, keepdims=True) + EPS) * gain_row


def norm_back(values, gain_row, upstream):
    inv_root = lax.rsqrt(jnp.mean(values * values, axis=-1, keepdims=True) + EPS)
    normed = values * inv_root
    gain_grad = jnp.sum(upstream * normed, axis=0)
    inner_grad = upstream * gain_row
    grad_in = inv_root * (
        inner_grad - normed * jnp.mean(inner_grad * normed, axis=-1, keepdims=True)
    )
    return (grad_in, gain_grad)


def rope_tables(length, width):
    half_width = width // 2
    frequency = jnp.exp(
        -jnp.arange(half_width, dtype=jnp.float32) * (2.0 * math.log(10000.0) / width)
    )
    angles = jnp.arange(length, dtype=jnp.float32)[:, None] * frequency[None, :]
    return (jnp.cos(angles), jnp.sin(angles))


def rotate(values, cosine_table, sine_table):
    half_width = values.shape[-1] // 2
    front_half = values[..., :half_width]
    back_half = values[..., half_width:]
    cos_b = cosine_table[:, None, :]
    sin_b = sine_table[:, None, :]
    return jnp.concatenate(
        [front_half * cos_b - back_half * sin_b, back_half * cos_b + front_half * sin_b], axis=-1
    )


def factors(a_part, b_all, cosine_table, sine_table, head_count):
    a_part = a_part.reshape(a_part.shape[0], head_count, RQ + 2 * RK)
    b_all = b_all.reshape(b_all.shape[0], RQ + 2 * RK, DH)
    b_query = rotate(b_all[:, :RQ], cosine_table, sine_table)
    b_key = rotate(b_all[:, RQ : RQ + RK], cosine_table, sine_table)
    b_value = b_all[:, RQ + RK :]
    queries = jnp.einsum("nhr,nrd->nhd", a_part[:, :, :RQ], b_query, precision=HIGH) / RQ
    keys_all = jnp.einsum("nhr,nrd->nhd", a_part[:, :, RQ : RQ + RK], b_key, precision=HIGH) / RK
    values_all = jnp.einsum("nhr,nrd->nhd", a_part[:, :, RQ + RK :], b_value, precision=HIGH) / RK
    return (queries, keys_all, values_all)


def block_scores(query_blk, keys_bf, start_row, block_len, length):
    scores = jnp.einsum(
        "qhd,khd->hqk", query_blk, keys_bf, preferred_element_type=jnp.float32
    ) * DH ** (-0.5)
    places = jnp.arange(keys_bf.shape[0])
    query_pos = start_row + jnp.arange(block_len)
    allowed = (places[None, :] <= query_pos[:, None]) & (places[None, :] < length)
    return jnp.where(allowed[None], scores, NEG)


def attend(queries_bf, keys_bf, values_bf, length, block_len):

    def one_block(block_index):
        start_row = block_index * block_len
        query_blk = lax.dynamic_slice_in_dim(queries_bf, start_row, block_len, 0)
        scores = block_scores(query_blk, keys_bf, start_row, block_len, length)
        row_peak = jnp.max(scores, axis=-1, keepdims=True)
        shifted = jnp.exp(scores - row_peak)
        row_total = jnp.sum(shifted, axis=-1, keepdims=True)
        soft_bf = (shifted / row_total).astype(jnp.bfloat16)
        mixed_blk = jnp.einsum(
            "hqk,khd->qhd", soft_bf, values_bf, preferred_element_type=jnp.float32
        )
        return (mixed_blk.astype(jnp.bfloat16), (row_peak + jnp.log(row_total))[..., 0])

    mixed_all, log_total = lax.map(one_block, jnp.arange(queries_bf.shape[0] // block_len))
    return (mixed_all.reshape(queries_bf.shape), log_total)


def attend_back(queries_bf, keys_bf, values_bf, log_total, mixed_grad, length, block_len):

    def one_block(running, block_index):
        key_grad, value_grad = running
        start_row = block_index * block_len
        query_blk = lax.dynamic_slice_in_dim(queries_bf, start_row, block_len, 0)
        grad_blk = lax.dynamic_slice_in_dim(mixed_grad, start_row, block_len, 0)
        scores = block_scores(query_blk, keys_bf, start_row, block_len, length)
        soft_rows = jnp.exp(scores - log_total[block_index][:, :, None])
        prob_grad = jnp.einsum(
            "qhd,khd->hqk", grad_blk, values_bf, preferred_element_type=jnp.float32
        )
        score_grad = soft_rows * (
            prob_grad - jnp.sum(soft_rows * prob_grad, axis=-1, keepdims=True)
        )
        score_bf = score_grad.astype(jnp.bfloat16)
        query_grad = jnp.einsum(
            "hqk,khd->qhd", score_bf, keys_bf, preferred_element_type=jnp.float32
        ) * DH ** (-0.5)
        key_grad = key_grad + jnp.einsum(
            "hqk,qhd->khd", score_bf, query_blk, preferred_element_type=jnp.float32
        ) * DH ** (-0.5)
        value_grad = value_grad + jnp.einsum(
            "hqk,qhd->khd",
            soft_rows.astype(jnp.bfloat16),
            grad_blk,
            preferred_element_type=jnp.float32,
        )
        return ((key_grad, value_grad), query_grad)

    zeros_kv = jnp.zeros(keys_bf.shape, jnp.float32)
    (key_grad, value_grad), query_grad = lax.scan(
        one_block, (zeros_kv, zeros_kv), jnp.arange(queries_bf.shape[0] // block_len)
    )
    return (query_grad.reshape(queries_bf.shape), key_grad, value_grad)


def combine_softmax(left_part, right_part):
    peak_left, total_left, pick_left = left_part
    peak_right, total_right, pick_right = right_part
    new_peak = jnp.maximum(peak_left, peak_right)
    new_total = total_left * jnp.exp(peak_left - new_peak) + total_right * jnp.exp(
        peak_right - new_peak
    )
    return (new_peak, new_total, pick_left + pick_right)


def adam_update(weight, first, second, gradient, step_rate, decay_rate):
    first_new = BETA_ONE * first + (1.0 - BETA_ONE) * gradient
    second_new = BETA_TWO * second + (1.0 - BETA_TWO) * gradient * gradient
    first_hat = first_new / (1.0 - BETA_ONE**STEP)
    second_hat = second_new / (1.0 - BETA_TWO**STEP)
    weight_new = weight - step_rate * (
        first_hat / (jnp.sqrt(second_hat) + ADAM_EPS) + decay_rate * weight
    )
    return (weight_new, first_new, second_new)


def mat(left_op, right_op):
    return jnp.dot(left_op, right_op, preferred_element_type=jnp.float32)


def head_total(values):
    return lax.psum(values, "head")


def keep_same(values):
    return values


def per_device(
    token_ids,
    next_target,
    second_target,
    live_mask,
    row_lengths,
    tables,
    factor_head,
    factor_shared,
    project_out,
    feed_in,
    feed_out,
    norm_gains,
    tables_first,
    factor_head_first,
    factor_shared_first,
    project_out_first,
    feed_in_first,
    feed_out_first,
    norm_gains_first,
    tables_second,
    factor_head_second,
    factor_shared_second,
    project_out_second,
    feed_in_second,
    feed_out_second,
    norm_gains_second,
):
    bf16 = jnp.bfloat16
    head_index = lax.axis_index("head")
    vocab_local = tables.shape[1]
    offset = head_index * vocab_local
    tokens = token_ids[0]
    length = row_lengths[0]
    seq_len = tokens.shape[0]
    places = jnp.arange(seq_len)
    live_float = live_mask[0].astype(jnp.float32)
    live_both = jnp.stack(
        [
            live_float * (places < length - 1).astype(jnp.float32),
            live_float * (places < length - 2).astype(jnp.float32),
        ]
    )
    counts = lax.psum(jnp.sum(live_both, axis=1), "batch")
    table_full, head_full, shared_full, out_full, feed_in_full, feed_out_full, gain_full = (
        lax.all_gather(tables.astype(bf16), "batch", axis=2, tiled=True),
        lax.all_gather(factor_head.astype(bf16), "batch", axis=0, tiled=True),
        lax.all_gather(factor_shared.astype(bf16), "batch", axis=0, tiled=True),
        lax.all_gather(project_out.astype(bf16), "batch", axis=1, tiled=True),
        lax.all_gather(feed_in.astype(bf16), "batch", axis=1, tiled=True),
        lax.all_gather(feed_out.astype(bf16), "batch", axis=1, tiled=True),
        lax.all_gather(norm_gains.astype(bf16), "batch", axis=1, tiled=True),
    )
    local_ids = tokens - offset
    inside = (local_ids >= 0) & (local_ids < vocab_local)
    picked = jnp.take(table_full[0], jnp.clip(local_ids, 0, vocab_local - 1), axis=0)
    embed_part = jnp.where(inside[:, None], picked, jnp.zeros_like(picked))
    head_tables = table_full[1:]
    stream_in = lax.psum(embed_part, "head").astype(jnp.float32)
    reduce_term, spread_rows, stream_base = (head_total, keep_same, stream_in)
    gain_rows = gain_full.astype(jnp.float32)
    heads_here = head_full.shape[1] // (RQ + 2 * RK)
    cosine_table, sine_table = rope_tables(seq_len, DH)
    block_len = min(512, seq_len)
    normed_one = rms_norm(stream_in, gain_rows[0]).astype(bf16)
    head_coef = mat(normed_one, head_full)
    shared_coef = mat(normed_one, shared_full)
    queries, keys_all, values_all = factors(
        head_coef, shared_coef, cosine_table, sine_table, heads_here
    )
    queries_bf, keys_bf, values_bf = (
        queries.astype(bf16),
        keys_all.astype(bf16),
        values_all.astype(bf16),
    )
    mixed_heads, log_total = attend(queries_bf, keys_bf, values_bf, length, block_len)
    mixed_flat = mixed_heads.reshape(seq_len, heads_here * DH)
    stream_mid = stream_base + reduce_term(mat(mixed_flat, out_full))
    normed_two = spread_rows(rms_norm(stream_mid, gain_rows[1]).astype(bf16))
    gate_act = mat(normed_two, feed_in_full[0])
    up_act = mat(normed_two, feed_in_full[1])
    hidden = (jax.nn.silu(gate_act) * up_act).astype(bf16)
    stream_top = stream_mid + reduce_term(mat(hidden, feed_out_full))
    normed_top = spread_rows(rms_norm(stream_top, gain_rows[2]).astype(bf16))
    logits = jnp.einsum("nd,jvd->jnv", normed_top, head_tables, preferred_element_type=jnp.float32)
    targets = jnp.stack([next_target[0], second_target[0]]) - offset
    target_in = (targets >= 0) & (targets < vocab_local)
    target_pos = jnp.clip(targets, 0, vocab_local - 1)
    local_peak = jnp.max(logits, axis=-1)
    local_total = jnp.sum(jnp.exp(logits - local_peak[..., None]), axis=-1)
    local_pick = jnp.where(
        target_in, jnp.take_along_axis(logits, target_pos[..., None], axis=-1)[..., 0], 0.0
    )
    vocab_peak, vocab_total, target_logit = joined(
        (local_peak, local_total, local_pick), "head", combine_softmax
    )
    vocab_lse = vocab_peak + jnp.log(vocab_total)
    token_weight = live_both / counts[:, None]
    loss_local = jnp.sum(token_weight * (vocab_lse - target_logit))
    softmax_vocab = jnp.exp(logits - vocab_lse[..., None])
    onehot = (jnp.arange(vocab_local)[None, None, :] == target_pos[..., None]) & target_in[
        ..., None
    ]
    logit_grad = ((softmax_vocab - onehot.astype(jnp.float32)) * token_weight[..., None]).astype(
        bf16
    )
    top_in_grad = reduce_term(
        jnp.einsum("jnv,jvd->nd", logit_grad, head_tables, preferred_element_type=jnp.float32)
    )
    head_table_grad = jnp.einsum(
        "jnv,nd->jvd", logit_grad, normed_top, preferred_element_type=jnp.float32
    )
    grad_top, gain_top = norm_back(stream_top, gain_rows[2], top_in_grad)
    feed_grad_bf = spread_rows(grad_top.astype(bf16))
    feed_out_grad = mat(hidden.T, feed_grad_bf)
    hidden_grad = mat(feed_grad_bf, feed_out_full.T)
    sigmoid_gate = jax.nn.sigmoid(gate_act)
    gate_grad = (
        hidden_grad * up_act * sigmoid_gate * (1.0 + gate_act * (1.0 - sigmoid_gate))
    ).astype(bf16)
    up_grad = (hidden_grad * gate_act * sigmoid_gate).astype(bf16)
    feed_in_grad = jnp.stack([mat(normed_two.T, gate_grad), mat(normed_two.T, up_grad)])
    two_grad = reduce_term(mat(gate_grad, feed_in_full[0].T) + mat(up_grad, feed_in_full[1].T))
    branch_grad, gain_two = norm_back(stream_mid, gain_rows[1], two_grad)
    grad_mid = grad_top + branch_grad
    attn_grad_bf = spread_rows(grad_mid.astype(bf16))
    out_grad = mat(mixed_flat.T, attn_grad_bf)
    mixed_grad = mat(attn_grad_bf, out_full.T).astype(bf16).reshape(seq_len, heads_here, DH)
    query_grad, key_grad, value_grad = attend_back(
        queries_bf, keys_bf, values_bf, log_total, mixed_grad, length, block_len
    )
    _, factor_pull = jax.vjp(
        lambda a_part, b_all: factors(a_part, b_all, cosine_table, sine_table, heads_here),
        head_coef,
        shared_coef,
    )
    coef_grad, shared_part = factor_pull((query_grad, key_grad, value_grad))
    coef_bf = coef_grad.astype(bf16)
    one_part, shared_sum = (
        lax.psum(mat(coef_bf, head_full.T).astype(jnp.bfloat16), "head").astype(jnp.float32),
        lax.psum(shared_part.astype(jnp.bfloat16), "head").astype(jnp.float32),
    )
    shared_bf = shared_sum.astype(bf16)
    one_grad = one_part + mat(shared_bf, shared_full.T)
    head_weight_grad = mat(normed_one.T, coef_bf)
    shared_weight_grad = mat(normed_one.T, shared_bf)
    in_part, gain_one = norm_back(stream_in, gain_rows[0], one_grad)
    grad_in = grad_mid + in_part
    gain_grads = jnp.stack([gain_one, gain_two, gain_top])
    segment_ids = jnp.where(inside, local_ids, vocab_local)
    embed_grad = jax.ops.segment_sum(grad_in, segment_ids, num_segments=vocab_local + 1)[
        :vocab_local
    ]
    table_grad = jnp.concatenate([embed_grad[None], head_table_grad], axis=0)
    table_red, head_red, shared_red, out_red, feed_in_red, feed_out_red, gain_red = (
        lax.psum_scatter(
            table_grad.astype(jnp.bfloat16), "batch", scatter_dimension=2, tiled=True
        ).astype(jnp.float32),
        lax.psum_scatter(
            head_weight_grad.astype(jnp.bfloat16), "batch", scatter_dimension=0, tiled=True
        ).astype(jnp.float32),
        lax.psum_scatter(
            shared_weight_grad.astype(jnp.bfloat16), "batch", scatter_dimension=0, tiled=True
        ).astype(jnp.float32),
        lax.psum_scatter(
            out_grad.astype(jnp.bfloat16), "batch", scatter_dimension=1, tiled=True
        ).astype(jnp.float32),
        lax.psum_scatter(
            feed_in_grad.astype(jnp.bfloat16), "batch", scatter_dimension=1, tiled=True
        ).astype(jnp.float32),
        lax.psum_scatter(
            feed_out_grad.astype(jnp.bfloat16), "batch", scatter_dimension=1, tiled=True
        ).astype(jnp.float32),
        lax.psum_scatter(
            gain_grads.astype(jnp.bfloat16), "batch", scatter_dimension=1, tiled=True
        ).astype(jnp.float32),
    )
    grads = (table_red, head_red, shared_red, out_red, feed_in_red, feed_out_red, gain_red)
    owner_flag = (head_index == 0).astype(jnp.float32)
    squares = jnp.zeros((), jnp.float32)
    for i in range(7):
        partial_sq = jnp.sum(grads[i] * grads[i])
        squares = squares + (partial_sq if OWNED[i] else partial_sq * owner_flag)
    square_total, loss_total = lax.psum((squares, loss_local * owner_flag), ("batch", "head"))
    grad_norm = jnp.sqrt(square_total)
    clip_scale = jnp.minimum(1.0, CLIP / grad_norm)
    params = (tables, factor_head, factor_shared, project_out, feed_in, feed_out, norm_gains)
    firsts = (
        tables_first,
        factor_head_first,
        factor_shared_first,
        project_out_first,
        feed_in_first,
        feed_out_first,
        norm_gains_first,
    )
    seconds = (
        tables_second,
        factor_head_second,
        factor_shared_second,
        project_out_second,
        feed_in_second,
        feed_out_second,
        norm_gains_second,
    )
    updated = [
        adam_update(params[i], firsts[i], seconds[i], grads[i] * clip_scale, RATES[i], DECAYS[i])
        for i in range(7)
    ]
    return (
        loss_total,
        grad_norm,
        updated[0][0],
        updated[0][1],
        updated[0][2],
        updated[1][0],
        updated[1][1],
        updated[1][2],
        updated[2][0],
        updated[2][1],
        updated[2][2],
        updated[3][0],
        updated[3][1],
        updated[3][2],
        updated[4][0],
        updated[4][1],
        updated[4][2],
        updated[5][0],
        updated[5][1],
        updated[5][2],
        updated[6][0],
        updated[6][1],
        updated[6][2],
    )


def solution(mesh):
    placed = (
        P("batch", None),
        P("batch", None),
        P("batch", None),
        P("batch", None),
        P("batch"),
        P(None, "head", "batch"),
        P("batch", "head"),
        P("batch", None),
        P("head", "batch"),
        P(None, "batch", "head"),
        P("head", "batch"),
        P(None, "batch"),
        P(None, "head", "batch"),
        P("batch", "head"),
        P("batch", None),
        P("head", "batch"),
        P(None, "batch", "head"),
        P("head", "batch"),
        P(None, "batch"),
        P(None, "head", "batch"),
        P("batch", "head"),
        P("batch", None),
        P("head", "batch"),
        P(None, "batch", "head"),
        P("head", "batch"),
        P(None, "batch"),
    )
    return jax.shard_map(
        per_device,
        mesh=mesh,
        in_specs=placed,
        out_specs=(
            P(),
            P(),
            P(None, "head", "batch"),
            P(None, "head", "batch"),
            P(None, "head", "batch"),
            P("batch", "head"),
            P("batch", "head"),
            P("batch", "head"),
            P("batch", None),
            P("batch", None),
            P("batch", None),
            P("head", "batch"),
            P("head", "batch"),
            P("head", "batch"),
            P(None, "batch", "head"),
            P(None, "batch", "head"),
            P(None, "batch", "head"),
            P("head", "batch"),
            P("head", "batch"),
            P("head", "batch"),
            P(None, "batch"),
            P(None, "batch"),
            P(None, "batch"),
        ),
        check_vma=False,
    )
```

profile of v0, /device:TPU:0, one launch (start us, length us, event | category | flops | bytes accessed | tf_op | source)
XLA Modules:
  0.0 3328.3 jit_solution(30496565041174108)
XLA Ops:
  20.0 238.8 %all-gather.8.cloned.1.call-done = bf16[3,6288,1024]{2,1,0:T(8,128)(2,1)} async-done(((bf16[3,6288,256]{2,1,0:T(8,128)(2,1)}), bf16[3,6288,1024]{2,1,0:T(8,128)(2,1)}) %all-gather.8.cloned.1.call-update) | async-done | bytes 38633488 | tf_op jit(solution)/shard_map/all_gather | solution.py:225
  312.7 134.5 %all-reduce.19.cloned.1.call-done = bf16[2048,1024]{1,0:T(8,128)(2,1)} async-done(((bf16[2048,1024]{1,0:T(8,128)(2,1)}), bf16[2048,1024]{1,0:T(8,128)(2,1)}) %all-reduce.19.cloned.1.call-update) | async-done | bytes 4194320 | tf_op jit(solution)/shard_map/psum | solution.py:238
  586.1 45.3 %while.41 = (s32[]{:T(128)}, bf16[4,512,2,64]{1,3,2,0:T(8,128)(2,1)S(1)}, f32[4,2,512]{2,1,0:T(2,128)}, s32[4]{0:T(128)S(1)}, s32[]{:T(128)}, /*index=5*/bf16[20...) while((s32[]{:T(128)}, ...), condition=%wide.region_7.8_spmd, body=%wide.region_4.7_spmd.sunk | while | flops 564200960 | bytes 30712512 | solution.py:106
  646.9 261.1 %all-reduce.21.cloned.1.call-done = f32[2048,1024]{1,0:T(8,128)} async-done(((f32[2048,1024]{1,0:T(8,128)}), f32[2048,1024]{1,0:T(8,128)}) %all-reduce.21.cloned.1.call-update) | async-done | bytes 8388624 | tf_op jit(solution)/shard_map/psum | solution.py:173
  953.2 260.2 %all-reduce.23.cloned.1.call-done = f32[2048,1024]{1,0:T(8,128)} async-done(((f32[2048,1024]{1,0:T(8,128)}), f32[2048,1024]{1,0:T(8,128)}) %all-reduce.23.cloned.1.call-update) | async-done | bytes 8388624 | tf_op jit(solution)/shard_map/psum | solution.py:173
  1223.5 65.6 %fusion.169 = (f32[2,2048]{1,0:T(2,128)S(1)}, f32[2,2048,6288]{1,2,0:T(8,128)}) fusion(bf16[3,6288,1024]{2,1,0:T(8,128)(2,1)} %all-gather.8.cloned.1.call-done, f32[2048,1024]{1,0:T(8,128)} %get-tuple-element.392, f32[1024]{0:T(1024)S(1)} %bitcast.220, f32[2048]{0:T(1024)S(1)} %add_rsqrt_fusion), kind=kOutput, calls=%fused_computation.283 | convolution fusion | flops 52779610112 | bytes 137195520 | tf_op jit(solution)/shard_map/nd,jvd->jnv/dot_general | solution.py:264
  1289.2 167.2 %gather_fusion.1 = f32[4096]{0:T(1024)S(1)} fusion(f32[2,2048,6288]{1,2,0:T(8,128)} %get-tuple-element.428, s32[4096]{0:T(1024)S(1)} %bitcast.196), kind=kCustom, calls=%fused_computation.1 | custom fusion | bytes 81920 | tf_op jit(solution)/shard_map/jit(take_along_axis)/gather | solution.py:271
  1456.6 30.6 all_gather.48
  1487.2 31.6 exponential_reduce_fusion
  1518.9 30.5 all-gather.3
  1549.4 30.7 all-gather.2
  1581.4 90.7 %fusion.65 = f32[2048,1024]{1,0:T(8,128)} fusion(bf16[3,6288,1024]{2,1,0:T(8,128)(2,1)} %all-gather.8.cloned.1.call-done, f32[2,2048,6288]{1,2,0:T(8,128)} %get-tuple-element.428, f32[2,2048]{1,0:T(2,128)S(1)} %get-tuple-element.390, s32[2,2048]{1,0:T(2,128)S(1)} %copy-done.89, f32[2,2048]{1,0:T(2,128)S(1)} %get-tuple-element.389, ...), kind=kOutput, calls=%fused_computation.115 | convolution fusion | flops 52927856640 | bytes 137220096 | tf_op jit(solution)/shard_map/jnv,jvd->nd/dot_general | solution.py:287
  1672.4 267.4 %all-reduce.25.cloned.1.call-done = f32[2048,1024]{1,0:T(8,128)} async-done(((f32[2048,1024]{1,0:T(8,128)}), f32[2048,1024]{1,0:T(8,128)}) %all-reduce.25.cloned.1.call-update) | async-done | bytes 8388624 | tf_op jit(solution)/shard_map/psum | solution.py:173
  1965.7 269.5 %all-reduce.27.cloned.1.call-done = f32[2048,1024]{1,0:T(8,128)} async-done(((f32[2048,1024]{1,0:T(8,128)}), f32[2048,1024]{1,0:T(8,128)}) %all-reduce.27.cloned.1.call-update) | async-done | bytes 8388624 | tf_op jit(solution)/shard_map/psum | solution.py:173
  2256.0 133.6 %while.43 = (s32[]{:T(128)}, f32[2048,2,64]{0,2,1:T(8,128)S(1)}, f32[2048,2,64]{0,2,1:T(8,128)}, f32[4,512,2,64]{1,3,2,0:T(8,128)}, s32[4]{0:T(128)S(1)}, /*inde...) while((s32[]{:T(128)}, f32[2048,2,64]{0,2,1:T(8,128)S(1)}, ...), condition=%wide.region_24.25_spmd.clone, body=%wide.region_22.24_spmd.clone.sunk | while | flops 1377109504 | bytes 115643248 | solution.py:141
  2571.2 81.5 %convolution_convert_fusion = bf16[2,6288,1024]{2,1,0:T(8,128)(2,1)} fusion(f32[2048,1024]{1,0:T(8,128)} %get-tuple-element.392, f32[1024]{0:T(1024)S(1)} %bitcast.223, f32[2048]{0:T(1024)S(1)} %copy-done.70, f32[2,2048,6288]{1,2,0:T(8,128)} %get-tuple-element.428, f32[2,2048]{1,0:T(2,128)S(1)} %copy-done.88, s32[2,2048]{1,0:T(2,128)S(1)} %copy-done.90, ...), kind=kOutput, calls=%fused_computation.77 | convolution fusion | flops 52947025920 | bytes 137232384 | tf_op jit(solution)/shard_map/jnv,nd->jvd/dot_general | solution.py:289
  2661.9 122.8 %all-reduce.29.cloned.1.call-done = (bf16[2048,1024]{1,0:T(8,128)(2,1)}, bf16[2048,640]{0,1:T(8,128)(2,1)}) async-done(((bf16[2048,1024]{1,0:T(8,128)(2,1)}, bf16[2048,640]{0,1:T(8,128)(2,1)}), (bf16[2048,1024]{1,0:T(8,128)(2,1)}, bf16[2048,640]{0,1:T(8,128)(2,1)})) %all-reduce.29.cloned.1.call-update) | async-done | bytes 6815760 | tf_op jit(solution)/shard_map/psum | solution.py:319
  2806.6 31.4 scatter_custom_fusion
  2851.6 26.0 pad_maximum_fusion
  2886.8 21.5 reduce-scatter.22.cloned.1.call-done
  2910.6 27.5 reduce-scatter.14.cloned.1.call-done
  2940.5 270.4 %reduce-scatter.10.cloned.1.call-done = bf16[3,6288,256]{2,1,0:T(8,128)(2,1)} async-done(((bf16[3,6288,1024]{2,1,0:T(8,128)(2,1)}), bf16[3,6288,256]{2,1,0:T(8,128)(2,1)}) %reduce-scatter.10.cloned.1.call-update) | async-done | bytes 9658384 | tf_op jit(solution)/shard_map/reduce_scatter | solution.py:335
  3223.6 39.6 %all-reduce.10 = (f32[]{:T(128)}, f32[]{:T(128)}) all-reduce(f32[]{:T(128)S(6)} %mul.882, f32[]{:T(128)S(6)} %add.389), channel_id=1, replica_groups=mesh['batch'=4,'head'=8] {'batch','head'}, use_global_device_ids=true, to_apply=%region_17.18 | all-reduce | flops 2 | bytes 16 | tf_op jit(solution)/shard_map/psum | solution.py:363
  3275.7 44.7 %multiply_subtract_fusion = (f32[3,6288,256]{2,1,0:T(8,128)}, f32[3,6288,256]{2,1,0:T(8,128)}, f32[3,6288,256]{2,1,0:T(8,128)}) fusion(f32[3,6288,256]{2,1,0:T(8,128)} %param.37, f32[]{:T(128)S(6)} %min.47, bf16[3,6288,256]{2,1,0:T(8,128)(2,1)} %reduce-scatter.10.cloned.1.call-done, f32[3,6288,256]{2,1,0:T(8,128)} %param.44, f32[3,6288,256]{2,1,0:T(8,128)} %param.51), kind=kLoop, calls=%fused_computation.76 | loop fusion | flops 82096128 | bytes 125558784 | tf_op jit(solution)/shard_map/sub | solution.py:162
  (511 shorter events, 747.7 us)
Async XLA Ops:
  7.2 251.6 %all-gather.8.cloned.1.call-start = ((), (), s32[]{:S(2)}) async-start(), calls=%async_computation.7 | async-start | bytes 48291840 | tf_op jit(solution)/shard_map/all_gather | solution.py:225
  18.6 428.6 %all-reduce.19.cloned.1.call-start = ((), (), s32[]{:S(2)}) async-start(), calls=%async_computation.8 | async-start | bytes 8388608 | tf_op jit(solution)/shard_map/psum | solution.py:238
  290.8 175.8 %all-gather.10.cloned.1.call-start = ((), (), s32[]{:S(2)}) async-start(), calls=%async_computation.9 | async-start | bytes 1638400 | tf_op jit(solution)/shard_map/all_gather | solution.py:227
  291.6 616.4 %all-reduce.21.cloned.1.call-start = ((), (), s32[]{:S(2)}) async-start(), calls=%async_computation.10 | async-start | bytes 16777216 | tf_op jit(solution)/shard_map/psum | solution.py:173
  637.5 290.6 %all-gather.12.cloned.1.call-start = ((), (), s32[]{:S(2)}) async-start(), calls=%async_computation.11 | async-start | bytes 1802240 | tf_op jit(solution)/shard_map/all_gather | solution.py:229
  638.4 575.0 %all-reduce.23.cloned.1.call-start = ((), (), s32[]{:S(2)}) async-start(), calls=%async_computation.12 | async-start | bytes 16777216 | tf_op jit(solution)/shard_map/psum | solution.py:173
  942.9 996.9 %all-reduce.25.cloned.1.call-start = ((), (), s32[]{:S(2)}) async-start(), calls=%async_computation.13 | async-start | bytes 16777216 | tf_op jit(solution)/shard_map/psum | solution.py:173
  1223.5 723.9 %copy-start.69 = (f32[2048]{0:T(1024)}, f32[2048]{0:T(1024)S(1)}, u32[]{:S(2)}) copy-start(f32[2048]{0:T(1024)S(1)} %add_rsqrt_fusion) | copy-start | bytes 24580
  1672.2 563.1 %all-reduce.27.cloned.1.call-start = ((), (), s32[]{:S(2)}) async-start(), calls=%async_computation.14 | async-start | bytes 16777216 | tf_op jit(solution)/shard_map/psum | solution.py:173
  1965.6 819.1 %all-reduce.29.cloned.1.call-start = ((), (), s32[]{:S(2)}) async-start(), calls=%async_computation.22 | async-start | bytes 13631488 | tf_op jit(solution)/shard_map/psum | solution.py:319
  2557.3 321.2 %reduce-scatter.20.cloned.1.call-start = ((), (), s32[]{:S(2)}) async-start(), calls=%async_computation.20 | async-start | bytes 901120 | tf_op jit(solution)/shard_map/reduce_scatter | solution.py:350
  2563.8 316.3 %reduce-scatter.18.cloned.1.call-start = ((), (), s32[]{:S(2)}) async-start(), calls=%async_computation.19 | async-start | bytes 1802240 | tf_op jit(solution)/shard_map/reduce_scatter | solution.py:347
  2571.0 311.0 %reduce-scatter.12.cloned.1.call-start = ((), (), s32[]{:S(2)}) async-start(), calls=%async_computation.16 | async-start | bytes 61440 | tf_op jit(solution)/shard_map/reduce_scatter | solution.py:338
  2656.8 228.6 %reduce-scatter.16.cloned.1.call-start = ((), (), s32[]{:S(2)}) async-start(), calls=%async_computation.18 | async-start | bytes 327680 | tf_op jit(solution)/shard_map/reduce_scatter | solution.py:344
  2661.7 246.7 %reduce-scatter.22.cloned.1.call-start = ((), (), s32[]{:S(2)}) async-start(), calls=%async_computation.21 | async-start | bytes 327680
  2799.1 139.0 %reduce-scatter.14.cloned.1.call-start = ((), (), s32[]{:S(2)}) async-start(), calls=%async_computation.17 | async-start | bytes 1638400 | tf_op jit(solution)/shard_map/reduce_scatter | solution.py:341
  2806.3 404.6 %reduce-scatter.10.cloned.1.call-start = ((), (), s32[]{:S(2)}) async-start(), calls=%async_computation.15 | async-start | bytes 48291840 | tf_op jit(solution)/shard_map/reduce_scatter | solution.py:335
  2877.6 386.3 %copy-start.92 = (f32[3,256]{1,0:T(4,128)S(1)}, f32[3,256]{1,0:T(4,128)}, u32[]{:S(2)}) copy-start(f32[3,256]{1,0:T(4,128)} %param.43) | copy-start | bytes 9220
  2877.6 387.7 %copy-start.47 = (f32[352,256]{1,0:T(8,128)S(1)}, f32[352,256]{1,0:T(8,128)}, u32[]{:S(2)}) copy-start(f32[352,256]{1,0:T(8,128)} %param.42) | copy-start | bytes 1081348
  2877.7 389.9 %copy-start.28 = (f32[2,256,352]{1,2,0:T(8,128)S(1)}, f32[2,256,352]{1,2,0:T(8,128)}, u32[]{:S(2)}) copy-start(f32[2,256,352]{1,2,0:T(8,128)} %param.41) | copy-start | bytes 2162692
  2877.7 389.9 %copy-start.53 = (f32[2,256,352]{1,2,0:T(8,128)S(1)}, f32[2,256,352]{1,2,0:T(8,128)}, u32[]{:S(2)}) copy-start(f32[2,256,352]{1,2,0:T(8,128)} %param.48) | copy-start | bytes 2162692
  2878.5 386.8 %copy-start.54 = (bf16[352,256]{1,0:T(8,128)(2,1)S(1)}, bf16[352,256]{1,0:T(8,128)(2,1)}, u32[]{:S(2)}) copy-start(bf16[352,256]{1,0:T(8,128)(2,1)} %reduce-scatter.20.cloned.1.call-done) | copy-start | bytes 540676
  2880.2 387.4 %copy-start.48 = (bf16[2,256,352]{1,2,0:T(8,128)(2,1)S(1)}, bf16[2,256,352]{1,2,0:T(8,128)(2,1)}, u32[]{:S(2)}) copy-start(bf16[2,256,352]{1,2,0:T(8,128)(2,1)} %reduce-scatter.18.cloned.1.call-done) | copy-start | bytes 1081348
  2940.5 331.6 %copy-start.32 = (f32[256,640]{1,0:T(8,128)S(1)}, f32[256,640]{1,0:T(8,128)}, u32[]{:S(2)}) copy-start(f32[256,640]{1,0:T(8,128)} %param.39) | copy-start | bytes 1966084
  (111 other events, 5471.6 us)
Sparse Core Ops, SparseCore 0:
  18.7 239.9 all-gather.7
  290.9 156.2 all-reduce.18
  449.3 17.1 all-gather.9
  637.6 270.3 all-reduce.20
  910.0 18.1 all-gather.11
  943.0 270.3 all-reduce.22
  1672.3 267.4 all-reduce.24
  1965.8 269.4 all-reduce.26
  2557.4 227.2 all-reduce.28
  2787.7 21.9 reduce-scatter.19
  2812.4 27.3 reduce-scatter.17
  2842.7 19.3 reduce-scatter.11
  2865.3 20.0 reduce-scatter.15
  2888.2 20.0 reduce-scatter.21
  2911.5 26.5 reduce-scatter.13
  2940.6 270.3 reduce-scatter.9
where the time goes:
time: 3340 us; the launch traced here: 3330 us
  waiting for transfers between devices  1900 us (57%)
  matrix products  601 us (18%)
  other arithmetic  321 us (10%)
  local copies, waits for them, and re-layouts  305 us (9%)
  blocking collectives  163 us (5%)
    psum x4, waiting for transfers between devices, head_total(): return lax.psum(values, 'head')  1060 us
    reduce_scatter x1, waiting for transfers between devices, per_device(): lax.psum_scatter(table_grad.astype(jnp.bfloat16), 'batch', scatter_dimens...  270 us
    all_gather x1, waiting for transfers between devices, per_device(): lax.all_gather(tables.astype(bf16), 'batch', axis=2, tiled=True)  239 us
    gather x2, local copies, waits for them, and re-layouts, per_device(): jnp.take_along_axis(logits, target_pos[..., None], axis=-1)[..., 0]  167 us
    psum x1, waiting for transfers between devices, per_device(): stream_in = lax.psum(embed_part, 'head').astype(jnp.float32)  134 us
    psum x1, waiting for transfers between devices, per_device(): lax.psum(mat(coef_bf, head_full.T).astype(jnp.bfloat16), 'head')  123 us
    all_gather x3, blocking collectives, joined(): pieces = jax.tree.map(lambda part: lax.all_gather(part, axis), value)  91.8 us
    dot_general x1, matrix products, per_device(): jnp.einsum('jnv,jvd->nd', logit_grad, head_tables, preferred_element_type...  90.7 us
  transfers between devices with their start and end apart: 16, of which 13 were waited for; matrix products, arithmetic and copies ran while one was open for 7% of the time, Pallas kernels for 0%

commit v1 on v0

v1 whole, which is shorter than its diff:
```python
import functools
import math

import jax
import jax.numpy as jnp
from jax import lax
from jax.experimental import pallas as pl
from jax.experimental.pallas import tpu as pltpu
from jax.sharding import PartitionSpec as P

DH = 64
RQ = 6
RK = 2
RT = RQ + 2 * RK
STEP = 10
EPS = 1e-05
NEG = -1e30
CLIP = 0.02
BETA_ONE = 0.9
BETA_TWO = 0.95
ADAM_EPS = 1e-08
RATES = (0.1, 0.1, 0.05, 0.2, 0.05, 0.03, 0.3)
DECAYS = (0.1, 0.1, 0.1, 0.1, 0.1, 0.1, 0.0)
OWNED = (True, True, False, True, True, True, False)
BF = jnp.bfloat16
F32 = jnp.float32
ALL = ("batch", "head")


def dot(left, right, contract_left, contract_right):
    return lax.dot_general(
        left, right, (((contract_left,), (contract_right,)), ((), ())),
        preferred_element_type=F32,
    )


def gather_small(values, axis, count):
    return lax.all_to_all(
        jnp.broadcast_to(values[None], (count,) + values.shape), axis, 0, 0
    )


def core_swap(values, count):
    return lax.ppermute(values, "batch", [(i, i ^ 1) for i in range(count)])


def swap(values, axis, count, step):
    return lax.ppermute(values, axis, [(i, i ^ step) for i in range(count)])


def bits(count):
    return [1 << i for i in range(count.bit_length() - 1)]


def by_distance(values, index):
    count = values.shape[0]
    shape = values.shape[1:]
    for step in bits(count):
        folded = values.reshape((count // (2 * step), 2, step) + shape)
        flip = ((index // step) % 2) == 1
        values = jnp.where(flip, folded[:, ::-1], folded).reshape((count,) + shape)
    return values


def batch_pieces(values, count):
    pieces = {0: values}
    for step in reversed(bits(count)):
        for k in list(pieces):
            pieces[k | step] = swap(pieces[k], "batch", count, step)
    return [pieces[k] for k in range(count)]


def batch_total(pieces, count):
    for step in bits(count):
        pieces = {
            k: pieces[k].astype(F32) + swap(pieces[k | step], "batch", count, step).astype(F32)
            for k in range(0, count, 2 * step)
        }
        if 2 * step < count:
            pieces = {k: part.astype(BF) for k, part in pieces.items()}
    return pieces[0]


def head_split(count):
    along_z = min(4, count)
    return along_z, count // along_z


def head_near(values, count):
    along_z, along_y = head_split(count)
    pieces = {0: values}
    for k in range(1, along_z):
        pieces[k * along_y] = swap(values, "head", count, k * along_y)
    for step in bits(along_y):
        for k in list(pieces):
            pieces[k | step] = swap(pieces[k], "head", count, step)
    return [pieces[k] for k in range(count)]


def head_total(pieces, count):
    along_z, along_y = head_split(count)
    for step in reversed(bits(along_y)):
        pieces = {
            k: (pieces[k].astype(F32) + swap(pieces[k | step], "head", count, step).astype(F32)).astype(BF)
            for k in range(count)
            if k % along_y < step
        }
    total = pieces[0].astype(F32)
    for k in range(1, along_z):
        total = total + swap(pieces[k * along_y], "head", count, k * along_y).astype(F32)
    return total


TILE = 256
CHUNK = 512


def vocab_blocks(vocab_local):
    block = vocab_local
    for parts in range(1, vocab_local + 1):
        if vocab_local % parts == 0 and vocab_local // parts <= 2112 and vocab_local // parts % 8 == 0:
            block = vocab_local // parts
            break
    edges = list(range(0, max(block - CHUNK // 2, 1), CHUNK)) + [block]
    return block, [(lo, hi - lo) for lo, hi in zip(edges[:-1], edges[1:])]


def table_chunk(table_refs, low, size):
    return jnp.concatenate([ref[0, low : low + size, :] for ref in table_refs], axis=-1)


def logits_kernel(nb, block, chunks, *refs):
    table_refs = refs[:nb]
    hf_ref, target_ref, e_ref, stat_ref = refs[nb:]
    first = pl.program_id(1) * block

    def one_tile(n, carry):
        cols = pl.ds(pl.multiple_of(n * TILE, TILE), TILE)
        rows = hf_ref[cols, :]
        target = target_ref[0, :, cols] - first
        for c, (low, size) in enumerate(chunks):
            logits = dot(table_chunk(table_refs, low, size), rows, 1, 1)
            peak = jnp.max(logits, axis=0, keepdims=True)
            shifted = jnp.exp(logits - peak)
            place = lax.broadcasted_iota(jnp.int32, logits.shape, 0)
            pick = jnp.where(place == target - low, logits, 0.0)
            e_ref[0, low : low + size, cols] = shifted.astype(BF)
            stat_ref[0, 0, 3 * c : 3 * c + 1, cols] = peak
            stat_ref[0, 0, 3 * c + 1 : 3 * c + 2, cols] = jnp.sum(shifted, axis=0, keepdims=True)
            stat_ref[0, 0, 3 * c + 2 : 3 * c + 3, cols] = jnp.sum(pick, axis=0, keepdims=True)
        return carry

    lax.fori_loop(0, hf_ref.shape[0] // TILE, one_tile, 0)


def logit_grad(e_ref, scale_ref, target, weight, c, low, size, cols):
    place = lax.broadcasted_iota(jnp.int32, (size, target.shape[1]), 0)
    soft = e_ref[0, low : low + size, cols].astype(F32) * scale_ref[0, 0, c : c + 1, cols]
    return (soft - jnp.where(place == target - low, weight, 0.0)).astype(BF)


def hidden_grad_kernel(nb, block, chunks, last, *refs):
    table_refs = refs[:nb]
    e_ref, scale_ref, target_ref, weight_ref, out_ref, total_ref = refs[nb:]
    first = pl.program_id(1) * block
    step = pl.program_id(0) * pl.num_programs(1) + pl.program_id(1)

    @pl.when(step == 0)
    def _():
        total_ref[...] = jnp.zeros_like(total_ref)

    def one_tile(n, carry):
        cols = pl.ds(pl.multiple_of(n * TILE, TILE), TILE)
        target = target_ref[0, :, cols] - first
        weight = weight_ref[0, :, cols]
        part = total_ref[cols, :]
        for c, (low, size) in enumerate(chunks):
            grad = logit_grad(e_ref, scale_ref, target, weight, c, low, size, cols)
            part = part + dot(grad, table_chunk(table_refs, low, size), 0, 0)
        total_ref[cols, :] = part
        return carry

    lax.fori_loop(0, total_ref.shape[0] // TILE, one_tile, 0)

    @pl.when(step == last)
    def _():
        out_ref[...] = total_ref[...].astype(out_ref.dtype)


def table_grad_kernel(nb, block, chunks, e_ref, scale_ref, target_ref, weight_ref, hf_ref, *out_refs):
    first = pl.program_id(1) * block
    d_local = out_refs[0].shape[2]
    every = slice(None)
    for c, (low, size) in enumerate(chunks):
        grad = logit_grad(
            e_ref, scale_ref, target_ref[0] - first, weight_ref[0], c, low, size, every
        )
        total = dot(grad, hf_ref[...], 1, 0).astype(BF)
        for k, ref in enumerate(out_refs):
            ref[0, low : low + size, :] = total[:, k * d_local : (k + 1) * d_local]


def attention_parts(a_ref, b_ref, q_ref, place_key_ref, place_query_ref):
    coef = a_ref[0]
    keys = ((coef[0:1] * b_ref[0] + coef[1:2] * b_ref[1]) / RK).astype(BF)
    values = ((coef[2:3] * b_ref[2] + coef[3:4] * b_ref[3]) / RK).astype(BF)
    scores = dot(q_ref[0], keys, 0, 0)
    scores = jnp.where(place_key_ref[...] <= place_query_ref[...], scores, NEG)
    shifted = jnp.exp(scores - jnp.max(scores, axis=1, keepdims=True))
    soft = shifted * (1.0 / jnp.sum(shifted, axis=1, keepdims=True))
    return keys, values, soft


def attend_kernel(a_ref, b_ref, q_ref, place_key_ref, place_query_ref, out_ref):
    _, values, soft = attention_parts(a_ref, b_ref, q_ref, place_key_ref, place_query_ref)
    out_ref[0] = dot(values, soft.astype(BF), 1, 1).astype(BF)


def attend_back_kernel(
    a_ref, b_ref, q_ref, place_key_ref, place_query_ref, grad_ref, dq_ref, da_ref, db_ref
):
    keys, values, soft = attention_parts(a_ref, b_ref, q_ref, place_key_ref, place_query_ref)
    grad = grad_ref[0]
    dprob = dot(grad, values, 0, 0)
    delta = jnp.sum(soft * dprob, axis=1, keepdims=True)
    dscore = (soft * (dprob - delta)).astype(BF)
    dq_ref[0] = dot(keys, dscore, 1, 1) * DH ** (-0.5)
    dkey = dot(q_ref[0], dscore, 1, 0) * (1.0 / RK)
    dvalue = dot(grad, soft.astype(BF), 1, 0) * (1.0 / RK)
    coef = a_ref[0]

    @pl.when(pl.program_id(0) == 0)
    def _():
        db_ref[...] = jnp.zeros_like(db_ref)

    for r, upstream in enumerate((dkey, dkey, dvalue, dvalue)):
        da_ref[0, r : r + 1, :] = jnp.sum(upstream * b_ref[r], axis=0, keepdims=True)
        db_ref[r] += upstream * coef[r : r + 1]


def attention_calls(heads, seq_len, own):
    a_spec = pl.BlockSpec((1, 2 * RK, seq_len), lambda h: (h, 0, 0))
    b_spec = pl.BlockSpec((2 * RK, DH, seq_len), lambda h: (0, 0, 0))
    q_spec = pl.BlockSpec((1, DH, own), lambda h: (h, 0, 0))
    key_spec = pl.BlockSpec((1, seq_len), lambda h: (0, 0))
    query_spec = pl.BlockSpec((own, 1), lambda h: (0, 0))
    params = pltpu.CompilerParams(vmem_limit_bytes=48 << 20)
    specs = [a_spec, b_spec, q_spec, key_spec, query_spec]
    cost = pl.CostEstimate(
        flops=32 * heads * own * seq_len * DH, bytes_accessed=24 * DH * seq_len, transcendentals=0
    )

    def attend(*operands):
        return pl.pallas_call(
            attend_kernel,
            grid=(heads,),
            in_specs=specs,
            out_specs=q_spec,
            out_shape=jax.ShapeDtypeStruct((heads, DH, own), BF),
            compiler_params=params,
            cost_estimate=cost,
        )(*operands)

    def attend_back(*operands):
        return pl.pallas_call(
            attend_back_kernel,
            grid=(heads,),
            in_specs=specs + [q_spec],
            out_specs=[q_spec, a_spec, b_spec],
            out_shape=[
                jax.ShapeDtypeStruct((heads, DH, own), F32),
                jax.ShapeDtypeStruct((heads, 2 * RK, seq_len), F32),
                jax.ShapeDtypeStruct((2 * RK, DH, seq_len), F32),
            ],
            compiler_params=params,
            cost_estimate=cost,
        )(*operands)

    return attend, attend_back


def head_calls(nb, vocab_local, d_local, seq_len):
    block, chunks = vocab_blocks(vocab_local)
    blocks = vocab_local // block
    width = nb * d_local
    grid = (2, blocks)
    table_spec = pl.BlockSpec((1, block, d_local), lambda j, v: (j, v, 0))
    whole = pl.BlockSpec((seq_len, width), lambda j, v: (0, 0))
    line = pl.BlockSpec((1, 1, seq_len), lambda j, v: (j, 0, 0))
    e_spec = pl.BlockSpec((1, block, seq_len), lambda j, v: (j, v, 0))
    stats = 3 * len(chunks)
    stat_spec = pl.BlockSpec((1, 1, stats, seq_len), lambda j, v: (j, v, 0, 0))
    scale_spec = pl.BlockSpec((1, 1, len(chunks), seq_len), lambda j, v: (j, v, 0, 0))
    params = pltpu.CompilerParams(vmem_limit_bytes=56 << 20)
    flops = 4 * vocab_local * seq_len * width
    cost = pl.CostEstimate(flops=flops, bytes_accessed=8 * vocab_local * (width + seq_len), transcendentals=0)

    def logits(pieces, hf, target):
        return pl.pallas_call(
            functools.partial(logits_kernel, nb, block, chunks),
            grid=grid,
            in_specs=[table_spec] * nb + [whole, line],
            out_specs=[e_spec, stat_spec],
            out_shape=[
                jax.ShapeDtypeStruct((2, vocab_local, seq_len), BF),
                jax.ShapeDtypeStruct((2, blocks, stats, seq_len), F32),
            ],
            compiler_params=params,
            cost_estimate=cost,
        )(*pieces, hf, target)

    def hidden_grad(pieces, e, scale, target, weight):
        return pl.pallas_call(
            functools.partial(hidden_grad_kernel, nb, block, chunks, 2 * blocks - 1),
            grid=grid,
            in_specs=[table_spec] * nb + [e_spec, scale_spec, line, line],
            out_specs=whole,
            out_shape=jax.ShapeDtypeStruct((seq_len, width), BF),
            scratch_shapes=[pltpu.VMEM((seq_len, width), F32)],
            compiler_params=params,
            cost_estimate=cost,
        )(*pieces, e, scale, target, weight)

    def table_grad(e, scale, target, weight, hf):
        return pl.pallas_call(
            functools.partial(table_grad_kernel, nb, block, chunks),
            grid=grid,
            in_specs=[e_spec, scale_spec, line, line, whole],
            out_specs=[table_spec] * nb,
            out_shape=[jax.ShapeDtypeStruct((2, vocab_local, d_local), BF)] * nb,
            compiler_params=params,
            cost_estimate=cost,
        )(e, scale, target, weight, hf)

    return logits, hidden_grad, table_grad


def total_all(values, counts):
    for axis, count in zip(ALL, counts):
        step = 1
        while step < count:
            values = values + lax.ppermute(
                values, axis, [(i, i ^ step) for i in range(count)]
            )
            step *= 2
    return values


def inv_rms(values):
    return lax.rsqrt(jnp.mean(values * values, axis=-1, keepdims=True) + EPS)


def norm_back(values, gain_row, upstream):
    inv_root = inv_rms(values)
    normed = values * inv_root
    gain_grad = jnp.sum(upstream * normed, axis=0)
    inner = upstream * gain_row
    grad_in = inv_root * (inner - normed * jnp.mean(inner * normed, axis=-1, keepdims=True))
    return (grad_in, gain_grad)


def device_order(row, heads):
    chunk = row.shape[-1] // (2 * heads)
    pieces = row.reshape(row.shape[:-1] + (2 * heads, chunk))
    front = pieces[..., :heads, :]
    back = pieces[..., heads:, :][..., ::-1, :]
    joined = jnp.concatenate([front, back], axis=-1)
    return joined


def turn(values, cosine, sine, sign):
    half = DH // 2
    front = values[..., :half, :]
    back = values[..., half:, :]
    if sign > 0:
        return jnp.concatenate([front * cosine - back * sine, back * cosine + front * sine], axis=-2)
    return jnp.concatenate([front * cosine + back * sine, back * cosine - front * sine], axis=-2)


def adam_update(weight, first, second, gradient, step_rate, decay_rate):
    first_new = BETA_ONE * first + (1.0 - BETA_ONE) * gradient
    second_new = BETA_TWO * second + (1.0 - BETA_TWO) * gradient * gradient
    first_hat = first_new / (1.0 - BETA_ONE**STEP)
    second_hat = second_new / (1.0 - BETA_TWO**STEP)
    weight_new = weight - step_rate * (
        first_hat / (jnp.sqrt(second_hat) + ADAM_EPS) + decay_rate * weight
    )
    return (weight_new, first_new, second_new)


def per_device(nb, nh, *args):
    (token_ids, next_target, second_target, live_mask, row_lengths) = args[:5]
    params, firsts, seconds = args[5:12], args[12:19], args[19:26]
    tables, factor_head, factor_shared, project_out, feed_in, feed_out, norm_gains = params
    head_index = lax.axis_index("head")
    core_index = lax.axis_index("batch") % 2
    vocab_local, d_local = tables.shape[1:]
    width = d_local * nb
    offset = head_index * vocab_local
    length = row_lengths[0]
    seq_len = token_ids.shape[1]
    own = seq_len // nh
    heads = factor_head.shape[1] * nh // RT
    ff_local = feed_out.shape[0]
    ff_half = ff_local // 2
    rows_out = project_out.shape[0]

    place_all = device_order(jnp.arange(seq_len), nh).reshape(seq_len)
    near = lambda rows: jnp.moveaxis(
        by_distance(jnp.moveaxis(rows.reshape(rows.shape[:-1] + (nh, own)), -2, 0), head_index), 0, -2
    ).reshape(rows.shape)
    place_own = lax.dynamic_slice_in_dim(place_all, head_index * own, own)
    ids_order = device_order(token_ids[0], nh)
    ids_all = gather_small(ids_order, "batch", nb)
    ids_own = lax.dynamic_index_in_dim(ids_order, head_index, 0, False)
    live_float = device_order(live_mask[0], nh).reshape(seq_len).astype(F32)
    live_both = jnp.stack(
        [
            live_float * (place_all < length - 1).astype(F32),
            live_float * (place_all < length - 2).astype(F32),
        ]
    )
    counts = jnp.sum(
        gather_small(jnp.sum(live_both, axis=1).reshape(1, 2), "batch", nb), axis=0
    ).reshape(2)
    token_weight = live_both / counts[:, None]

    batch_index = lax.axis_index("batch")
    gains = jnp.moveaxis(gather_small(norm_gains.astype(BF), "batch", nb), 0, 1).reshape(3, width).astype(F32)
    w_shared = gather_small(factor_shared.astype(BF), "batch", nb).reshape(width, RT * DH)
    w_head_part = gather_small(factor_head.astype(BF), "batch", nb).reshape(width, -1)
    w_head = gather_small(w_head_part.T, "head", nh).reshape(heads * RT, width)
    w_out_part = jnp.moveaxis(gather_small(project_out.astype(BF), "batch", nb), 0, 1).reshape(rows_out, width)
    feed_units = jnp.concatenate(
        [feed_in.astype(BF).transpose(0, 2, 1), feed_out.astype(BF)[None]], axis=0
    )
    feed_units = gather_small(feed_units, "batch", nb)
    feed_units = lax.dynamic_slice_in_dim(feed_units, core_index * ff_half, ff_half, 2)
    feed_units = jnp.moveaxis(feed_units, 0, 2).reshape(3 * ff_half, width)
    packed = lax.all_gather(jnp.concatenate([feed_units, w_out_part], axis=0), "head")
    feed_all = packed[:, : 3 * ff_half].reshape(nh, 3, ff_half, width)
    w_gate = feed_all[:, 0].reshape(nh * ff_half, width)
    w_up = feed_all[:, 1].reshape(nh * ff_half, width)
    w_down = feed_all[:, 2].reshape(nh * ff_half, width)
    w_out = packed[:, 3 * ff_half :].reshape(nh * rows_out, width)

    slots = max(16, 3 * own // 8 // 16 * 16)
    local_ids = ids_all - offset
    inside = (local_ids >= 0) & (local_ids < vocab_local)
    rank = jnp.cumsum(inside.astype(jnp.int32), axis=-1) - 1
    holder = jnp.arange(nh)[:, None]
    from_holder = (ids_own // vocab_local)[None, :] == holder
    rank_own = jnp.sum(
        jnp.where(from_holder, jnp.cumsum(from_holder.astype(jnp.int32), axis=1) - 1, 0), axis=0
    )
    most = jnp.max(
        jnp.sum(((ids_all // vocab_local)[:, :, None] == holder).astype(jnp.int32), axis=-1)
    )
    rounds = (most + slots - 1) // slots
    flat_tables = tables.reshape(3 * vocab_local, d_local)

    def round_ids(turn_index):
        wanted = turn_index * slots + jnp.arange(slots)
        match = (rank[:, :, None] == wanted[:, None]) & inside[:, :, None]
        found = jnp.sum(jnp.where(match, local_ids[:, :, None], 0), axis=-1)
        return jnp.where(jnp.any(match, axis=-1), found, vocab_local)

    def round_places(turn_index):
        wanted = (turn_index * slots + jnp.arange(slots))[None, None, :]
        match = from_holder.T[:, :, None] & (rank_own[:, None, None] == wanted)
        return match.astype(BF).reshape(own, nh * slots)

    def look_up(turn_index):
        picked = jnp.take(flat_tables, jnp.minimum(round_ids(turn_index).reshape(-1), vocab_local - 1), axis=0)
        shares = lax.all_to_all(picked.astype(BF).reshape(nb * nh, slots, d_local), ALL, 0, 0)
        shares = jnp.moveaxis(shares.reshape(nb, nh * slots, d_local), 0, 1).reshape(nh * slots, width)
        return dot(round_places(turn_index), shares, 1, 0)

    def give_back(turn_index, rows):
        sent = dot(round_places(turn_index), rows, 0, 0).astype(BF)
        sent = jnp.moveaxis(sent.reshape(nh, slots, nb, d_local), 2, 0).reshape(nb * nh, slots, d_local)
        shares = lax.all_to_all(sent, ALL, 0, 0).reshape(nb * nh * slots, d_local)
        return jax.ops.segment_sum(
            shares.astype(F32), round_ids(turn_index).reshape(-1), num_segments=vocab_local + 1
        )[:vocab_local]

    def all_rounds(one_round):
        return lax.fori_loop(1, rounds, lambda i, total: total + one_round(i), one_round(0))

    x0, head_tables = lax.optimization_barrier((all_rounds(look_up), tables[1:].astype(BF)))
    table_pieces = batch_pieces(head_tables, nb)

    h1 = (x0 * inv_rms(x0) * gains[0]).astype(BF)
    coef = dot(w_head, h1, 1, 1).reshape(heads, RT, own)
    shared = dot(w_shared, h1, 0, 1).reshape(RT, DH, own)
    frequency = jnp.exp(-jnp.arange(DH // 2, dtype=F32) * (2.0 * math.log(10000.0) / DH))
    angles = frequency[:, None] * place_own.astype(F32)[None, :]
    cosine, sine = jnp.cos(angles), jnp.sin(angles)
    b_query = turn(shared[:RQ], cosine, sine, 1)
    b_key = turn(shared[RQ : RQ + RK], cosine, sine, 1)
    b_value = shared[RQ + RK :]
    queries = sum(coef[:, r][:, None, :] * b_query[r][None] for r in range(RQ)) / RQ
    q_bf = (queries * DH ** (-0.5)).astype(BF)
    na = heads * 2 * RK
    kv_own = jnp.concatenate(
        [
            coef[:, RQ:].reshape(na, own),
            b_key.reshape(RK * DH, own),
            b_value.reshape(RK * DH, own),
        ],
        axis=0,
    )
    kv_all = jnp.concatenate(head_near(kv_own, nh), axis=1)
    a_all = kv_all[:na].reshape(heads, 2 * RK, seq_len)
    b_all = kv_all[na:].reshape(2 * RK, DH, seq_len)
    place_near = near(place_all)
    place_key = jnp.where(place_near < length, place_near, 2 * seq_len).reshape(1, seq_len)
    attend, attend_back = attention_calls(heads, seq_len, own)
    operands = (a_all, b_all, q_bf, place_key, place_own.reshape(own, 1))
    mixed = attend(*operands)
    mixed = mixed.reshape(heads * DH, own)
    x1 = x0 + dot(mixed, w_out, 0, 0)

    h2 = (x1 * inv_rms(x1) * gains[1]).astype(BF)
    h2_pair = jnp.concatenate([h2, core_swap(h2, nb)], axis=0)
    gate = dot(h2_pair, w_gate, 1, 1)
    up = dot(h2_pair, w_up, 1, 1)
    sig = jax.nn.sigmoid(gate)
    hidden = (gate * sig * up).astype(BF)
    down = dot(hidden, w_down, 1, 0)
    x2 = x1 + down[:own] + core_swap(down[own:], nb)

    hf = (x2 * inv_rms(x2) * gains[2]).astype(BF)
    hf = by_distance(hf.reshape(own, nb, d_local).swapaxes(0, 1), batch_index).swapaxes(0, 1).reshape(own, width)
    hf_all = jnp.concatenate(head_near(hf, nh), axis=0)

    call_logits, call_hidden, call_table = head_calls(nb, vocab_local, d_local, seq_len)
    targets = jnp.stack([device_order(next_target[0], nh), device_order(second_target[0], nh)])
    targets = near(targets.reshape(2, 1, seq_len)) - offset
    weight_near = near(token_weight)
    e_all, stats = call_logits(table_pieces, hf_all, targets)
    stats = stats.reshape(2, stats.shape[1], -1, 3, seq_len)
    peak_c = stats[:, :, :, 0]
    peak_l = jnp.max(peak_c, axis=(1, 2))
    total_l = jnp.sum(stats[:, :, :, 1] * jnp.exp(peak_c - peak_l[:, None, None]), axis=(1, 2))
    pick_l = jnp.sum(stats[:, :, :, 2], axis=(1, 2))
    found = gather_small(near(jnp.stack([peak_l, total_l, pick_l])), "head", nh)
    peak_g = jnp.max(found[:, 0], axis=0)
    total_g = jnp.sum(found[:, 1] * jnp.exp(found[:, 0] - peak_g), axis=0)
    lse = peak_g + jnp.log(total_g)
    loss_local = jnp.sum(token_weight * (lse - jnp.sum(found[:, 2], axis=0)))
    scale_c = jnp.exp(peak_c - near(lse)[:, None, None]) * weight_near[:, None, None]
    weight_line = weight_near.reshape(2, 1, seq_len)
    dhf_part = call_hidden(table_pieces, e_all, scale_c, targets, weight_line)
    dhf = head_total([dhf_part[k * own : (k + 1) * own] for k in range(nh)], nh)
    dhf = by_distance(dhf.reshape(own, nb, d_local).swapaxes(0, 1), batch_index).swapaxes(0, 1).reshape(own, width)
    dhf, table_grads = lax.optimization_barrier(
        (dhf, tuple(call_table(e_all, scale_c, targets, weight_line, hf_all)))
    )
    head_red = batch_total(table_grads, nb)

    dx2, gain_top = norm_back(x2, gains[2], dhf)
    e_own = dx2.astype(BF)
    e_pair = jnp.concatenate([e_own, core_swap(e_own, nb)], axis=0)
    dhidden = dot(e_pair, w_down, 1, 1)
    dgate = (dhidden * up * sig * (1.0 + gate * (1.0 - sig))).astype(BF)
    dup = (dhidden * gate * sig).astype(BF)
    g_gate = dot(dgate, h2_pair, 0, 0)
    g_up = dot(dup, h2_pair, 0, 0)
    g_down = dot(hidden, e_pair, 0, 0)
    dh2_pair = dot(dgate, w_gate, 1, 0) + dot(dup, w_up, 1, 0)
    dh2 = dh2_pair[:own] + core_swap(dh2_pair[own:], nb)
    back2, gain_two = norm_back(x1, gains[1], dh2)
    dx1 = dx2 + back2

    c_own = dx1.astype(BF)
    g_out = dot(mixed, c_own, 1, 0)
    g_feed = jnp.stack([g_gate, g_up, g_down]).astype(BF).reshape(3, nh, ff_half, width)
    g_pack = jnp.concatenate(
        [
            jnp.moveaxis(g_feed, 0, 1).reshape(nh, 3 * ff_half, width),
            g_out.astype(BF).reshape(nh, rows_out, width),
        ],
        axis=1,
    )
    g_pack = lax.psum_scatter(g_pack, "head", scatter_dimension=0)
    g_pack = lax.all_to_all(
        jnp.moveaxis(g_pack.reshape(3 * ff_half + rows_out, nb, d_local), 1, 0), "batch", 0, 0
    ).astype(F32)
    red_feed = jnp.sum(
        g_pack[:, : 3 * ff_half].reshape(nb // 2, 2, 3, ff_half, d_local), axis=0
    )
    red_feed = jnp.moveaxis(red_feed, 0, 1).reshape(3, ff_local, d_local)
    feed_in_red = red_feed[:2].transpose(0, 2, 1)
    feed_out_red = red_feed[2]
    out_red = jnp.sum(g_pack[:, 3 * ff_half :], axis=0)

    dmixed = dot(w_out, c_own, 1, 1).astype(BF).reshape(heads, DH, own)
    dq, da_kv, db_kv = attend_back(*operands, dmixed)
    dkv = jnp.concatenate([da_kv.reshape(na, seq_len), db_kv.reshape(2 * RK * DH, seq_len)], axis=0).astype(BF)
    dkv = head_total([dkv[:, k * own : (k + 1) * own] for k in range(nh)], nh)
    da_q = jnp.stack([jnp.sum(dq * b_query[r][None], axis=1) for r in range(RQ)], axis=1) / RQ
    db_q = jnp.stack([jnp.sum(dq * coef[:, r][:, None, :], axis=0) for r in range(RQ)]) / RQ
    dcoef = jnp.concatenate([da_q, dkv[:na].reshape(heads, 2 * RK, own)], axis=1)
    dcoef = dcoef.reshape(heads * RT, own).astype(BF)
    dshared = jnp.concatenate(
        [
            turn(db_q, cosine, sine, -1),
            turn(dkv[na : na + RK * DH].reshape(RK, DH, own), cosine, sine, -1),
            dkv[na + RK * DH :].reshape(RK, DH, own),
        ],
        axis=0,
    ).reshape(RT * DH, own).astype(BF)
    dh1 = dot(dcoef, w_head, 0, 0) + dot(dshared, w_shared, 0, 1)
    back1, gain_one = norm_back(x0, gains[0], dh1)
    dx0 = (dx1 + back1).astype(BF)

    g_coef = dot(h1, dcoef, 0, 1)
    g_shared = dot(h1, dshared, 0, 1)
    g_gain = jnp.stack([gain_one, gain_two, gain_top]).T
    g_small = jnp.concatenate([g_coef, g_shared, g_gain], axis=1).astype(BF)
    cols = g_small.shape[1]
    g_small = lax.all_to_all(g_small.reshape(nb, d_local, cols), "batch", 0, 0)
    g_small = jnp.sum(g_small.astype(F32), axis=0).astype(BF)
    g_small = lax.all_to_all(g_small.reshape(nh, d_local // nh, cols), "head", 0, 0)
    g_small = jnp.sum(g_small.astype(F32), axis=0).astype(BF)
    g_small = gather_small(g_small, "head", nh).reshape(d_local, cols).astype(F32)
    nc = heads * RT
    head_red_f = lax.dynamic_slice_in_dim(g_small[:, :nc], head_index * (nc // nh), nc // nh, 1)
    shared_red = g_small[:, nc : nc + RT * DH]
    gain_red = g_small[:, nc + RT * DH :].T

    embed_red = all_rounds(lambda turn_index: give_back(turn_index, dx0))

    grads = (None, head_red_f, shared_red, out_red, feed_in_red, feed_out_red, gain_red)
    owner_flag = (head_index == 0).astype(F32)
    squares = jnp.sum(embed_red * embed_red) + jnp.sum(head_red * head_red)
    for i in range(1, 7):
        part = jnp.sum(grads[i] * grads[i])
        squares = squares + (part if OWNED[i] else part * owner_flag)
    both = total_all(jnp.stack([squares, loss_local * owner_flag]).reshape(1, 2), (nb, nh))
    grad_norm = jnp.sqrt(both[0, 0])
    scale = jnp.minimum(1.0, CLIP / grad_norm)
    table_grad = jnp.concatenate([embed_red[None], head_red], axis=0)
    grads = (table_grad,) + grads[1:]
    outs = [both[0, 1], grad_norm]
    for i in range(7):
        outs.extend(
            adam_update(params[i], firsts[i], seconds[i], grads[i] * scale, RATES[i], DECAYS[i])
        )
    return tuple(outs)


def solution(mesh):
    nb, nh = mesh.shape["batch"], mesh.shape["head"]
    row = P("batch", None)
    weights = (
        P(None, "head", "batch"),
        P("batch", "head"),
        P("batch", None),
        P("head", "batch"),
        P(None, "batch", "head"),
        P("head", "batch"),
        P(None, "batch"),
    )
    return jax.shard_map(
        lambda *args: per_device(nb, nh, *args),
        mesh=mesh,
        in_specs=(row, row, row, row, P("batch")) + weights * 3,
        out_specs=(P(), P()) + tuple(spec for spec in weights for _ in range(3)),
        check_vma=False,
    )
```

time: 3340 us -> 1320 us (0.40)
  waiting for transfers between devices: 1900 us -> 509 us
  matrix products: 601 us -> 37.9 us
  Pallas kernels: 0 us -> 308 us
  local copies, waits for them, and re-layouts: 305 us -> 135 us
  blocking collectives: 163 us -> 6.09 us
  other arithmetic: 321 us -> 190 us
  starting transfers between devices: 1.26 us -> 102 us
    psum x6 -> x0, waiting for transfers between devices: 1320 us -> none  [the longest x4 1060 us: head_total(): return lax.psum(values, 'head')]
    dot_general x58 -> x20, matrix products: 601 us -> 37.9 us  [dot(): lax.dot_general(left, right, (((contract_left,), (contract_right,)), ((),...]
    pallas_call x0 -> x5, Pallas kernels: none -> 308 us  [the longest x1 97.2 us: logits(): pl.pallas_call(functools.partial(logits_kernel, nb, block, chunks), grid=...]
    all_gather x3 -> x1, waiting for transfers between devices: 264 us -> 25.9 us  [per_device(): lax.all_gather(jnp.concatenate([feed_units, w_out_part], axis=0), 'head')]
    ppermute x0 -> x43, waiting for transfers between devices: none -> 233 us  [the longest x34 215 us: swap(): return lax.ppermute(values, axis, [(i, i ^ step) for i in range(count)])]
    reduce_scatter x6 -> x1, waiting for transfers between devices: 300 us -> 70.3 us  [per_device(): g_pack = lax.psum_scatter(g_pack, 'head', scatter_dimension=0)]
    all_to_all x0 -> x14, waiting for transfers between devices: none -> 180 us  [the longest x1 69 us: give_back(): shares = lax.all_to_all(sent, ALL, 0, 0).reshape(nb * nh * slots, d_local)]
    gather x3 -> x1, local copies, waits for them, and re-layouts: 185 us -> 16.3 us  [look_up(): jnp.take(flat_tables, jnp.minimum(round_ids(turn_index).reshape(-1), voca...]
  transfers between devices with their start and end apart: 16 -> 59, of which waited for: 13 -> 39; matrix products, arithmetic and copies ran while one was open for 7% -> 18% of each run, Pallas kernels for 0% -> 10%
where the time goes in v1:
time: 1320 us; the launch traced here: 1310 us
  waiting for transfers between devices  509 us (39%)
  Pallas kernels  308 us (23%)
  other arithmetic  190 us (14%)
  local copies, waits for them, and re-layouts  135 us (10%)
  starting transfers between devices  102 us (8%)
  matrix products  37.9 us (3%)
  between operations  26.2 us (2%)
    ppermute x34, waiting for transfers between devices, swap(): return lax.ppermute(values, axis, [(i, i ^ step) for i in range(count)])  215 us
    pallas_call x1, Pallas kernels, logits(): pl.pallas_call(functools.partial(logits_kernel, nb, block, chunks), grid=...  97.2 us
    pallas_call x1, Pallas kernels, hidden_grad(): pl.pallas_call(functools.partial(hidden_grad_kernel, nb, block, chunks, 2...  76.9 us
    reduce_scatter x1, waiting for transfers between devices, per_device(): g_pack = lax.psum_scatter(g_pack, 'head', scatter_dimension=0)  70.3 us
    all_to_all x1, waiting for transfers between devices, give_back(): shares = lax.all_to_all(sent, ALL, 0, 0).reshape(nb * nh * slots, d_local)  69 us
    all_to_all x9, waiting for transfers between devices, gather_small(): lax.all_to_all(jnp.broadcast_to(values[None], (count,) + values.shape), a...  66.4 us
    pallas_call x1, Pallas kernels, table_grad(): pl.pallas_call(functools.partial(table_grad_kernel, nb, block, chunks), g...  60.7 us
    sub x7, other arithmetic, adam_update(): weight - step_rate * (first_hat / (jnp.sqrt(second_hat) + ADAM_EPS) + dec...  55.9 us
  transfers between devices with their start and end apart: 59, of which 39 were waited for; matrix products, arithmetic and copies ran while one was open for 18% of the time, Pallas kernels for 10%

profile of v1, /device:TPU:0, one launch (start us, length us, event | category | flops | bytes accessed | tf_op | source)
XLA Modules:
  0.0 1314.1 jit_solution(11875492567106924764)
XLA Ops:
  8.0 11.6 bitcast_convert_fusion.2
  67.2 16.3 %gather_fusion.1 = bf16[3072,256]{1,0:T(8,128)(2,1)S(1)} fusion(f32[18864,256]{1,0:T(8,128)} %bitcast.443, s32[3072]{0:T(1024)S(1)} %broadcast_clamp_fusion.1), kind=kCustom, calls=%fused_computation.1 | custom fusion | bytes 3158016 | tf_op jit(solution)/shard_map/jit(_take)/gather | solution.py:474
  106.3 31.4 %all-to-all-done.3 = bf16[32,96,256]{2,1,0:T(8,128)(2,1)S(1)} async-done(((bf16[32,96,256]{2,1,0:T(8,128)(2,1)}), bf16[32,96,256]{2,1,0:T(8,128)(2,1)S(1)}, u32[]{:S(2)}, u32[]{:S(2)}) %all-to-all-start.3) | async-done | bytes 1572896 | tf_op jit(solution)/shard_map/all_to_all | solution.py:475
  165.4 13.0 all-to-all-done.7
  196.5 22.0 %collective-permute-done.1 = f32[320,256]{0,1:T(8,128)S(1)} collective-permute-done((f32[320,256]{0,1:T(8,128)}, f32[320,256]{0,1:T(8,128)S(1)}, u32[]{:S(2)}, u32[]{:S(2)}) %collective-permute-start.1) | collective-permute-done | bytes 327712 | tf_op jit(solution)/shard_map/ppermute | solution.py:48
  221.1 13.2 %collective-permute-done.5 = f32[320,256]{0,1:T(8,128)S(1)} collective-permute-done((f32[320,256]{0,1:T(8,128)}, f32[320,256]{0,1:T(8,128)S(1)}, u32[]{:S(2)}, u32[]{:S(2)}) %collective-permute-start.5) | collective-permute-done | bytes 327712 | tf_op jit(solution)/shard_map/ppermute | solution.py:48
  239.9 15.3 %collective-permute-done.4 = f32[320,256]{0,1:T(8,128)S(1)} collective-permute-done((f32[320,256]{0,1:T(8,128)S(1)}, f32[320,256]{0,1:T(8,128)S(1)}, u32[]{:S(2)}, u32[]{:S(2)}) %collective-permute-start.4) | collective-permute-done | bytes 327712 | tf_op jit(solution)/shard_map/ppermute | solution.py:48
  256.8 14.1 %collective-permute-done.6 = f32[320,256]{0,1:T(8,128)S(1)} collective-permute-done((f32[320,256]{0,1:T(8,128)S(1)}, f32[320,256]{0,1:T(8,128)S(1)}, u32[]{:S(2)}, u32[]{:S(2)}) %collective-permute-start.6) | collective-permute-done | bytes 327712 | tf_op jit(solution)/shard_map/ppermute | solution.py:48
  281.4 27.6 %shard_map.425 = bf16[16,64,256]{2,1,0:T(8,128)(2,1)S(1)} custom-call(f32[16,4,2048]{2,1,0:T(4,128)S(1)} %copy-done.3, f32[4,64,2048]{2,1,0:T(8,128)S(1)} %bitcast.439, bf16[16,64,256]{2,1,0:T(8,128)(2,1)S(1)} %multiply_convert_fusion.5.q_ref, s32[1,2048]{1,0:T(1,128)S(1)} %compare_select_fusion.3.place_key_ref, s32[256,1]{1,0:T(8,128)S(1)} %copy.501.place_query_ref), custom_call_target="tpu_custom_call" | custom-call | flops 17179869184 | bytes 3145728 | tf_op jit(solution)/shard_map/pallas_call | solution.py:254
  309.1 25.9 %all-gather.3.cloned.1.call-done = bf16[5248,1024]{1,0:T(8,128)(2,1)} async-done(((bf16[656,1024]{1,0:T(8,128)(2,1)}), bf16[5248,1024]{1,0:T(8,128)(2,1)}) %all-gather.3.cloned.1.call-update) | async-done | bytes 10747920 | tf_op jit(solution)/shard_map/all_gather | solution.py:440
  437.0 97.2 %shard_map.426 = (bf16[2,6288,2048]{2,1,0:T(8,128)(2,1)}, f32[2,3,12,2048]{3,2,1,0:T(8,128)}) custom-call(bf16[2,6288,256]{2,1,0:T(8,128)(2,1)} %slice.672.refs_0_, bf16[2,6288,256]{2,1,0:T(8,128)(2,1)} %collective-permute-done.9.refs_1_, bf16[2,6288,256]{2,1,0:T(8,128)(2,1)} %collective-permute-done.10.refs_2_, ...), custom_call_target="tpu_custom_call" | custom-call | flops 52747567104 | bytes 154533888 | tf_op jit(solution)/shard_map/pallas_call | solution.py:299
  556.0 76.9 %shard_map.427 = bf16[2048,1024]{1,0:T(8,128)(2,1)} custom-call(bf16[2,6288,256]{2,1,0:T(8,128)(2,1)} %slice.672.refs_0_, bf16[2,6288,256]{2,1,0:T(8,128)(2,1)} %collective-permute-done.9.refs_1_, bf16[2,6288,256]{2,1,0:T(8,128)(2,1)} %collective-permute-done.10.refs_2_, bf16[2,6288,256]{2,1,0:T(8,128)(2,1)} %collective-permute-done.11.refs_3_, ...), custom_call_target="tpu_custom_call" | custom-call | flops 52747567104 | bytes 154533888 | tf_op jit(solution)/shard_map/pallas_call | solution.py:313
  650.4 11.2 collective-permute-done.24
  661.7 11.2 collective-permute-done.22
  678.1 60.7 %shard_map.428 = (bf16[2,6288,256]{2,1,0:T(8,128)(2,1)}, bf16[2,6288,256]{2,1,0:T(8,128)(2,1)}, bf16[2,6288,256]{2,1,0:T(8,128)(2,1)}, bf16[2,6288,256]{2,1,0:T(8,128)(2,1)}) custom-call(bf16[2,6288,2048]{2,1,0:T(8,128)(2,1)} %get-tuple-element.138.refs_4_.e_ref, f32[2,3,4,2048]{3,2,1,0:T(4,128)} %exponential_multiply_fusion.refs_5_.scale_ref, ...), custom_call_target="tpu_custom_call" | custom-call | flops 52747567104 | bytes 154533888 | tf_op jit(solution)/shard_map/pallas_call | solution.py:325
  777.0 45.1 %shard_map.429 = (f32[16,64,256]{2,1,0:T(8,128)S(1)}, f32[16,4,2048]{2,1,0:T(4,128)S(1)}, f32[4,64,2048]{2,1,0:T(8,128)S(1)}) custom-call(f32[16,4,2048]{2,1,0:T(4,128)S(1)} %copy-done.4, f32[4,64,2048]{2,1,0:T(8,128)} %bitcast.440, bf16[16,64,256]{2,1,0:T(8,128)(2,1)S(1)} %multiply_convert_fusion.5.q_ref, s32[1,2048]{1,0:T(1,128)S(1)} %compare_select_fusion.3.place_key_ref, ...), custom_call_target="tpu_custom_call" | custom-call | flops 17179869184 | bytes 3145728 | tf_op jit(solution)/shard_map/pallas_call | solution.py:265
  884.9 12.1 all-to-all-done.13
  929.9 17.0 %all-to-all-done.15 = bf16[8,32,803]{2,1,0:T(8,128)(2,1)} async-done(((bf16[8,32,803]{2,1,0:T(8,128)(2,1)}), bf16[8,32,803]{2,1,0:T(8,128)(2,1)}, u32[]{:S(2)}, u32[]{:S(2)}) %all-to-all-start.15) | async-done | bytes 411168 | tf_op jit(solution)/shard_map/all_to_all | solution.py:38
  957.3 69.0 %all-to-all-done.12 = bf16[32,96,256]{2,1,0:T(8,128)(2,1)S(1)} async-done(((bf16[32,96,256]{2,1,0:T(8,128)(2,1)}), bf16[32,96,256]{2,1,0:T(8,128)(2,1)S(1)}, u32[]{:S(2)}, u32[]{:S(2)}) %all-to-all-start.12) | async-done | bytes 1572896 | tf_op jit(solution)/shard_map/all_to_all | solution.py:482
  1026.3 22.7 %scatter_custom_fusion.1 = f32[6289,256]{1,0:T(8,128)} fusion(s32[3072]{0:T(1024)S(1)} %reshape.1008, f32[]{:T(128)} %constant.332.clone.1, bf16[3072,256]{1,0:T(8,128)(2,1)S(1)} %bitcast.471), kind=kCustom, calls=%fused_computation.59 | custom fusion | flops 1572864 | bytes 8012804 | tf_op jit(solution)/shard_map/scatter-add | solution.py:483
  1071.4 70.3 %reduce-scatter.2.cloned.1.call-done = bf16[1,656,1024]{2,1,0:T(8,128)(2,1)} async-done(((bf16[8,656,1024]{2,1,0:T(8,128)(2,1)}), bf16[1,656,1024]{2,1,0:T(8,128)(2,1)}) %reduce-scatter.2.cloned.1.call-update) | async-done | bytes 1343504 | tf_op jit(solution)/shard_map/reduce_scatter | solution.py:586
  1149.4 56.8 %collective-permute-done.37 = bf16[2,6288,256]{2,1,0:T(8,128)(2,1)} collective-permute-done((bf16[2,6288,256]{2,1,0:T(8,128)(2,1)}, bf16[2,6288,256]{2,1,0:T(8,128)(2,1)}, u32[]{:S(2)}, u32[]{:S(2)}) %collective-permute-start.37) | collective-permute-done | bytes 6438944 | tf_op jit(solution)/shard_map/ppermute | solution.py:48
  1206.2 13.8 %multiply_reduce_fusion = (f32[]{:T(128)}, f32[2,6288,256]{2,1,0:T(8,128)}) fusion(bf16[2,6288,256]{2,1,0:T(8,128)(2,1)} %collective-permute-done.37, bf16[2,6288,256]{2,1,0:T(8,128)(2,1)} %collective-permute-done.35, bf16[2,6288,256]{2,1,0:T(8,128)(2,1)} %get-tuple-element.149), kind=kLoop, calls=%fused_computation.42 | loop fusion | flops 28975104 | bytes 32194564 | tf_op jit(solution)/shard_map/reduce_sum | solution.py:637
  1259.0 46.9 %multiply_subtract_fusion = (f32[3,6288,256]{2,1,0:T(8,128)}, f32[3,6288,256]{2,1,0:T(8,128)}, f32[3,6288,256]{2,1,0:T(8,128)}) fusion(f32[3,6288,256]{2,1,0:T(8,128)} %param.35, f32[]{:T(128)S(6)} %min.43, f32[2,6288,256]{2,1,0:T(8,128)} %get-tuple-element.484, f32[1,6288,256]{2,1,0:T(8,128)} %bitcast.442, f32[3,6288,256]{2,1,0:T(8,128)} %param.42, ...), kind=kLoop, calls=%fused_computation.39 | loop fusion | flops 82096128 | bytes 135217152 | tf_op jit(solution)/shard_map/sub | solution.py:385
  (696 shorter events, 486.4 us)
Async XLA Ops:
  62.5 30.9 %all-to-all-start.8 = ((bf16[4,3,352,256]{3,2,1,0:T(8,128)(2,1)}), bf16[4,3,352,256]{3,2,1,0:T(8,128)(2,1)}, u32[]{:S(2)}, u32[]{:S(2)}) async-start(bf16[4,3,352,256]{3,2,1,0:T(8,128)(2,1)} %broadcast_in_dim.122), calls=%async_computation.8 | async-start | bytes 4325376 | tf_op jit(solution)/shard_map/all_to_all | solution.py:38
  93.5 44.3 %all-to-all-start.3 = ((bf16[32,96,256]{2,1,0:T(8,128)(2,1)}), bf16[32,96,256]{2,1,0:T(8,128)(2,1)S(1)}, u32[]{:S(2)}, u32[]{:S(2)}) async-start(bf16[32,96,256]{2,1,0:T(8,128)(2,1)} %select_convert_fusion.1), calls=%async_computation.3 | async-start | bytes 3145728 | tf_op jit(solution)/shard_map/all_to_all | solution.py:475
  142.6 192.4 %all-gather.3.cloned.1.call-start = ((), (), s32[]{:S(2)}) async-start(), calls=%async_computation.19 | async-start | bytes 12091392 | tf_op jit(solution)/shard_map/all_gather | solution.py:440
  163.1 175.7 %collective-permute-start.10 = (bf16[2,6288,256]{2,1,0:T(8,128)(2,1)}, bf16[2,6288,256]{2,1,0:T(8,128)(2,1)}, u32[]{:S(2)}, u32[]{:S(2)}) collective-permute-start(bf16[2,6288,256]{2,1,0:T(8,128)(2,1)} %slice.672.refs_0_), channel_id=1, source_target_pairs={{0,16},{8,24},{16,0},{24,8},{1,17},{9,25},{17,1},{25,9},{2,18},{10... | collective-permute-start | bytes 19316744 | tf_op jit(solution)/shard_map/ppermute | solution.py:48
  190.1 45.8 %collective-permute-start = (f32[320,256]{0,1:T(8,128)}, f32[320,256]{0,1:T(8,128)S(1)}, u32[]{:S(2)}, u32[]{:S(2)}) collective-permute-start(f32[320,256]{0,1:T(8,128)} %get-tuple-element.531), channel_id=1, source_target_pairs={{0,1},{1,0},{2,3},{3,2},{4,5},{5,4},{6,7},{7,6},{8,9},{9,8},{10,11... | collective-permute-start | bytes 983048 | tf_op jit(solution)/shard_map/ppermute | solution.py:48
  191.6 28.9 %collective-permute-start.3 = (f32[320,256]{0,1:T(8,128)}, f32[320,256]{0,1:T(8,128)S(1)}, u32[]{:S(2)}, u32[]{:S(2)}) collective-permute-start(f32[320,256]{0,1:T(8,128)} %get-tuple-element.531), channel_id=1, source_target_pairs={{0,4},{1,5},{2,6},{3,7},{4,0},{5,1},{6,2},{7,3},{8,12},{9,13},{10,... | collective-permute-start | bytes 983048 | tf_op jit(solution)/shard_map/ppermute | solution.py:48
  193.6 40.7 %collective-permute-start.5 = (f32[320,256]{0,1:T(8,128)}, f32[320,256]{0,1:T(8,128)S(1)}, u32[]{:S(2)}, u32[]{:S(2)}) collective-permute-start(f32[320,256]{0,1:T(8,128)} %get-tuple-element.531), channel_id=1, source_target_pairs={{0,6},{1,7},{2,4},{3,5},{4,2},{5,3},{6,0},{7,1},{8,14},{9,15},{10,... | collective-permute-start | bytes 983048 | tf_op jit(solution)/shard_map/ppermute | solution.py:48
  220.5 34.7 %collective-permute-start.4 = (f32[320,256]{0,1:T(8,128)S(1)}, f32[320,256]{0,1:T(8,128)S(1)}, u32[]{:S(2)}, u32[]{:S(2)}) collective-permute-start(f32[320,256]{0,1:T(8,128)S(1)} %collective-permute-done.3), channel_id=1, source_target_pairs={{0,1},{1,0},{2,3},{3,2},{4,5},{5,4},{6,7},{7,6},{8,9},{9,8},{10,11... | collective-permute-start | bytes 983048 | tf_op jit(solution)/shard_map/ppermute | solution.py:48
  234.3 36.6 %collective-permute-start.6 = (f32[320,256]{0,1:T(8,128)S(1)}, f32[320,256]{0,1:T(8,128)S(1)}, u32[]{:S(2)}, u32[]{:S(2)}) collective-permute-start(f32[320,256]{0,1:T(8,128)S(1)} %collective-permute-done.5), channel_id=1, source_target_pairs={{0,1},{1,0},{2,3},{3,2},{4,5},{5,4},{6,7},{7,6},{8,9},{9,8},{10,11... | collective-permute-start | bytes 983048 | tf_op jit(solution)/shard_map/ppermute | solution.py:48
  338.2 96.7 %collective-permute-start.9 = (bf16[2,6288,256]{2,1,0:T(8,128)(2,1)}, bf16[2,6288,256]{2,1,0:T(8,128)(2,1)}, u32[]{:S(2)}, u32[]{:S(2)}) collective-permute-start(bf16[2,6288,256]{2,1,0:T(8,128)(2,1)} %slice.672.refs_0_), channel_id=1, source_target_pairs={{0,8},{8,0},{16,24},{24,16},{1,9},{9,1},{17,25},{25,17},{2,10},{10... | collective-permute-start | bytes 19316744 | tf_op jit(solution)/shard_map/ppermute | solution.py:48
  338.8 96.2 %collective-permute-start.11 = (bf16[2,6288,256]{2,1,0:T(8,128)(2,1)}, bf16[2,6288,256]{2,1,0:T(8,128)(2,1)}, u32[]{:S(2)}, u32[]{:S(2)}) collective-permute-start(bf16[2,6288,256]{2,1,0:T(8,128)(2,1)} %collective-permute-done.10.refs_2_), channel_id=1, source_target_pairs={{0,8},{8,0},{16,24},{24,16},{1,9},{9,1},{17,25},{25,17},{2,10},{10... | collective-permute-start | bytes 19316744 | tf_op jit(solution)/shard_map/ppermute | solution.py:48
  376.7 38.2 %collective-permute-start.15 = (bf16[256,1024]{1,0:T(8,128)(2,1)S(1)}, bf16[256,1024]{1,0:T(8,128)(2,1)S(1)}, u32[]{:S(2)}, u32[]{:S(2)}) collective-permute-start(bf16[256,1024]{1,0:T(8,128)(2,1)S(1)} %bitcast.492), channel_id=1, source_target_pairs={{0,4},{1,5},{2,6},{3,7},{4,0},{5,1},{6,2},{7,3},{8,12},{9,13},{10,... | collective-permute-start | bytes 1572872 | tf_op jit(solution)/shard_map/ppermute | solution.py:48
  637.6 35.3 %collective-permute-start.22 = (bf16[256,1024]{1,0:T(8,128)(2,1)S(1)}, bf16[256,1024]{1,0:T(8,128)(2,1)S(1)}, u32[]{:S(2)}, u32[]{:S(2)}) collective-permute-start(bf16[256,1024]{1,0:T(8,128)(2,1)S(1)} %get-tuple-element.505), channel_id=1, source_target_pairs={{0,1},{1,0},{2,3},{3,2},{4,5},{5,4},{6,7},{7,6},{8,9},{9,8},{10,11... | collective-permute-start | bytes 1572872 | tf_op jit(solution)/shard_map/ppermute | solution.py:48
  639.1 99.7 %collective-permute-start.19 = (bf16[256,1024]{1,0:T(8,128)(2,1)}, bf16[256,1024]{1,0:T(8,128)(2,1)S(1)}, u32[]{:S(2)}, u32[]{:S(2)}) collective-permute-start(bf16[256,1024]{1,0:T(8,128)(2,1)} %get-tuple-element.503), channel_id=1, source_target_pairs={{0,1},{1,0},{2,3},{3,2},{4,5},{5,4},{6,7},{7,6},{8,9},{9,8},{10,11... | collective-permute-start | bytes 1572872 | tf_op jit(solution)/shard_map/ppermute | solution.py:48
  673.6 65.2 %collective-permute-start.25 = (bf16[256,1024]{1,0:T(8,128)(2,1)S(1)}, bf16[256,1024]{1,0:T(8,128)(2,1)S(1)}, u32[]{:S(2)}, u32[]{:S(2)}) collective-permute-start(bf16[256,1024]{1,0:T(8,128)(2,1)S(1)} %get-tuple-element.508), channel_id=1, source_target_pairs={{0,6},{1,7},{2,4},{3,5},{4,2},{5,3},{6,0},{7,1},{8,14},{9,15},{10,... | collective-permute-start | bytes 1572872 | tf_op jit(solution)/shard_map/ppermute | solution.py:48
  674.8 63.9 %collective-permute-start.23 = (bf16[256,1024]{1,0:T(8,128)(2,1)S(1)}, bf16[256,1024]{1,0:T(8,128)(2,1)S(1)}, u32[]{:S(2)}, u32[]{:S(2)}) collective-permute-start(bf16[256,1024]{1,0:T(8,128)(2,1)S(1)} %get-tuple-element.509), channel_id=1, source_target_pairs={{0,4},{1,5},{2,6},{3,7},{4,0},{5,1},{6,2},{7,3},{8,12},{9,13},{10,... | collective-permute-start | bytes 1572872 | tf_op jit(solution)/shard_map/ppermute | solution.py:48
  676.1 62.7 %collective-permute-start.21 = (bf16[256,1024]{1,0:T(8,128)(2,1)S(1)}, bf16[256,1024]{1,0:T(8,128)(2,1)}, u32[]{:S(2)}, u32[]{:S(2)}) collective-permute-start(bf16[256,1024]{1,0:T(8,128)(2,1)S(1)} %get-tuple-element.507), channel_id=1, source_target_pairs={{0,2},{1,3},{2,0},{3,1},{4,6},{5,7},{6,4},{7,5},{8,10},{9,11},{10,... | collective-permute-start | bytes 1572872 | tf_op jit(solution)/shard_map/ppermute | solution.py:48
  765.1 289.9 %collective-permute-start.36 = (bf16[2,6288,256]{2,1,0:T(8,128)(2,1)}, bf16[2,6288,256]{2,1,0:T(8,128)(2,1)}, u32[]{:S(2)}, u32[]{:S(2)}) collective-permute-start(bf16[2,6288,256]{2,1,0:T(8,128)(2,1)} %get-tuple-element.152), channel_id=1, source_target_pairs={{0,8},{8,0},{16,24},{24,16},{1,9},{9,1},{17,25},{25,17},{2,10},{10... | collective-permute-start | bytes 19316744 | tf_op jit(solution)/shard_map/ppermute | solution.py:48
  903.6 238.0 %reduce-scatter.2.cloned.1.call-start = ((), (), s32[]{:S(2)}) async-start(), calls=%async_computation.18 | async-start | bytes 12091392 | tf_op jit(solution)/shard_map/reduce_scatter | solution.py:586
  917.4 29.4 %all-to-all-start.15 = ((bf16[8,32,803]{2,1,0:T(8,128)(2,1)}), bf16[8,32,803]{2,1,0:T(8,128)(2,1)}, u32[]{:S(2)}, u32[]{:S(2)}) async-start(bf16[8,32,803]{2,1,0:T(8,128)(2,1)} %broadcast_in_dim.127), calls=%async_computation.15 | async-start | bytes 917504 | tf_op jit(solution)/shard_map/all_to_all | solution.py:38
  946.8 79.5 %all-to-all-start.12 = ((bf16[32,96,256]{2,1,0:T(8,128)(2,1)}), bf16[32,96,256]{2,1,0:T(8,128)(2,1)S(1)}, u32[]{:S(2)}, u32[]{:S(2)}) async-start(bf16[32,96,256]{2,1,0:T(8,128)(2,1)} %bitcast.96), calls=%async_computation.12 | async-start | bytes 3145728 | tf_op jit(solution)/shard_map/all_to_all | solution.py:482
  952.1 197.2 %collective-permute-start.35 = (bf16[2,6288,256]{2,1,0:T(8,128)(2,1)}, bf16[2,6288,256]{2,1,0:T(8,128)(2,1)}, u32[]{:S(2)}, u32[]{:S(2)}) collective-permute-start(bf16[2,6288,256]{2,1,0:T(8,128)(2,1)} %get-tuple-element.150), channel_id=1, source_target_pairs={{0,8},{8,0},{16,24},{24,16},{1,9},{9,1},{17,25},{25,17},{2,10},{10... | collective-permute-start | bytes 19316744 | tf_op jit(solution)/shard_map/ppermute | solution.py:48
  1064.3 141.8 %collective-permute-start.37 = (bf16[2,6288,256]{2,1,0:T(8,128)(2,1)}, bf16[2,6288,256]{2,1,0:T(8,128)(2,1)}, u32[]{:S(2)}, u32[]{:S(2)}) collective-permute-start(bf16[2,6288,256]{2,1,0:T(8,128)(2,1)} %add_convert_fusion), channel_id=1, source_target_pairs={{0,16},{8,24},{16,0},{24,8},{1,17},{9,25},{17,1},{25,9},{2,18},{10... | collective-permute-start | bytes 19316744 | tf_op jit(solution)/shard_map/ppermute | solution.py:48
  1145.8 76.1 %all-to-all-start.16 = ((bf16[4,656,256]{2,1,0:T(8,128)(2,1)}), bf16[4,656,256]{2,1,0:T(8,128)(2,1)S(1)}, u32[]{:S(2)}, u32[]{:S(2)}) async-start(bf16[4,656,256]{2,1,0:T(8,128)(2,1)} %bitcast.381), calls=%async_computation.17 | async-start | bytes 2686976 | tf_op jit(solution)/shard_map/all_to_all | solution.py:587
  (167 other events, 2775.6 us)
Sparse Core Ops, SparseCore 0:
  146.2 188.8 all-gather.2
  915.4 226.2 reduce-scatter.1
